TPU v7x, 128 devices: a whole 4x4x4 slice. The times are simulated.
128 devices in a mesh: dp: 32 (over y, x, z_lo), tensor: 4 (over z_hi, core).
Axes of the slice: x: 4, y: 4, z: 4 (z_hi: 2, z_lo: 2; z = z_hi * 2 + z_lo), core: 2. Of those that a mesh axis runs over, the one named last changes fastest.
Arguments:
- hidden_in: bfloat16 [32768, 1536], P(('dp', 'tensor')), may hold values from -6 to 6
- norm_gain: float32 [1536], replicated, may hold values from 0.1 to 1.9
- proj_zx: bfloat16 [1536, 2, 3072], P('dp', None, 'tensor'), may hold values from -0.15625 to 0.15625
- proj_shared: bfloat16 [1536, 256], P(('dp', 'tensor')), may hold values from -0.15625 to 0.15625
- proj_step: bfloat16 [1536, 48], P('dp', 'tensor'), may hold values from -0.15625 to 0.15625
- conv_inner: float32 [5, 3072], P(None, 'tensor'), may hold values from -0.5 to 0.5
- conv_shared: float32 [5, 256], replicated, may hold values from -0.5 to 0.5
- step_bias: float32 [48], P('tensor'), may hold values from -6 to -2
- decay_log: float32 [48], P('tensor'), may hold values from 0 to 2.7
- skip_gain: float32 [48], P('tensor'), may hold values from 0.5 to 1.5
- gated_gain: float32 [3072], P('tensor'), may hold values from 0.1 to 1.9
- proj_out: bfloat16 [3072, 1536], P('tensor', 'dp'), may hold values from -0.109375 to 0.109375
- out_grad: bfloat16 [32768, 1536], P(('dp', 'tensor')), may hold values from -6 to 6
- segments: int32 [32768], P('dp'), may hold values from 0 to 6, as said below
Outputs:
- hidden_out: bfloat16 [32768, 1536], P(('dp', 'tensor'))
- grad_hidden: bfloat16 [32768, 1536], P(('dp', 'tensor'))
- grad_norm_gain: float32 [1536], replicated
- grad_proj_zx: float32 [1536, 2, 3072], P('dp', None, 'tensor')
- grad_proj_shared: float32 [1536, 256], P(('dp', 'tensor'))
- grad_proj_step: float32 [1536, 48], P('dp', 'tensor')
- grad_conv_inner: float32 [5, 3072], P(None, 'tensor')
- grad_conv_shared: float32 [5, 256], replicated
- grad_step_bias: float32 [48], P('tensor')
- grad_decay_log: float32 [48], P('tensor')
- grad_skip_gain: float32 [48], P('tensor')
- grad_gated_gain: float32 [3072], P('tensor')
- grad_proj_out: float32 [3072, 1536], P('tensor', 'dp')
Inputs may be any that keep to these rules, and one draw needn't show every extreme that they name: `segments`: within each sequence of 1024 tokens the ids start at 0 and never fall; a document is a run of equal ids.
All inputs are finite; a program needn't handle non-finite values.
Results may differ from a plain program's by a relative error of at most 0.024.
Values may be sent and summed in bfloat16 or wider, within the bound.
No kernel may reach another device: no remote copies, remote signals or barrier semaphores. Data moves between devices by JAX's collectives and lax.ppermute only.
A program may use at most 256 MiB of HBM per device.

v0:
```python
import jax
import jax.numpy as jnp
from jax import lax
from jax.experimental import pallas as pl
from jax.experimental.pallas import tpu as pltpu
from jax.sharding import Mesh
from jax.sharding import PartitionSpec as P

EPS = 1e-05
DP = ("y", "x", "zl")
TENSOR = ("zh", "c")
SIZES = {"y": 4, "x": 4, "zl": 2, "zh": 2, "c": 2}

F32 = jnp.float32
BF16 = jnp.bfloat16
HIGH = lax.Precision.HIGHEST
BLOCK = 128
VMEM = 56 * 1024 * 1024
PARAMS = pltpu.CompilerParams(vmem_limit_bytes=VMEM)
NT = (((1,), (1,)), ((), ()))
TN = (((0,), (0,)), ((), ()))
VMEM_SPEC = pl.BlockSpec(memory_space=pltpu.VMEM)


def cost(us):
    return pl.CostEstimate(flops=int(us * 1e6), transcendentals=0, bytes_accessed=int(us * 3e3))


def whole(shape):
    return pl.BlockSpec(shape, lambda *i: (0,) * len(shape))


def column_block(rows, width, index):
    return pl.BlockSpec((rows, width), lambda *i: (0, index))


def first_specs(rows):
    return [column_block(rows, 384, index) for index in (4, 5, 6)]


def dot(a, b):
    return jnp.dot(a, b, preferred_element_type=F32)


def dot_nt(a, b):
    return lax.dot_general(a, b, NT, preferred_element_type=F32)


def sigmoid(a):
    return 0.5 * jnp.tanh(0.5 * a) + 0.5


def softplus(a):
    return jnp.maximum(a, 0.0) + jnp.log1p(jnp.exp(-jnp.abs(a)))


def conv_strip(ext, taps, aux, j):
    n = ext.shape[0] - 8
    lanes = slice(j * 128, (j + 1) * 128)
    total = taps[4:5, lanes] + taps[3:4, lanes] * ext[8 : 8 + n, lanes]
    for back in (1, 2, 3):
        total += taps[3 - back : 4 - back, lanes] * (
            aux[:, back - 1 : back] * ext[8 - back : 8 - back + n, lanes]
        )
    return total


def spread_heads(cols, j, low_half):
    return jnp.where(low_half, cols[:, 2 * j : 2 * j + 1], cols[:, 2 * j + 1 : 2 * j + 2])


def scan_forward_kernel(tok, weights_a, weights_b, weights_c, taps, heads, chan, aux, segrow, pre_out, scan_out, state_out, ext, act, carry, fed):
    n = tok.shape[0]
    pairs = carry.shape[1] // 128

    @pl.when(pl.program_id(0) == 0)
    def _():
        carry[...] = jnp.zeros_like(carry)
        ext[0:8, :] = jnp.zeros((8, ext.shape[1]), F32)

    pre = jnp.concatenate([dot(tok[...], w[...]) for w in (weights_a, weights_b, weights_c)], 1)
    pre_out[...] = pre
    wide = ext.shape[1]
    ext[8:, :] = pre[:, :wide]
    marks = aux[...]
    for j in range(wide // 128):
        total = conv_strip(ext, taps, marks, j)
        act[:, j * 128 : (j + 1) * 128] = total * sigmoid(total)
    ext[0:8, :] = ext[n : n + 8, :]

    step = softplus(pre[:, wide:] + heads[0:1, :])
    log_step = -step * heads[1:2, :]
    row = lax.broadcasted_iota(jnp.int32, (n, n), 0)
    col = lax.broadcasted_iota(jnp.int32, (n, n), 1)
    lower = (row >= col).astype(F32)
    cum = jnp.dot(lower, log_step, precision=HIGH, preferred_element_type=F32)
    cum_t = cum.T
    write = act[:, pairs * 128 : (pairs + 1) * 128]
    read = act[:, (pairs + 1) * 128 : (pairs + 2) * 128].astype(BF16)
    write_t = write.T.astype(BF16)
    allowed = (row >= col) & (marks[:, 8:9] == segrow[0:1, :])
    inner = jnp.where(allowed, dot(read, write_t), 0.0)
    last = cum[n - 1 : n, :]
    enters = jnp.exp(cum) * marks[:, 3:4]
    to_end = jnp.exp(last - cum) * marks[:, 4:5]
    keep = jnp.exp(last) * marks[n - 1 : n, 3:4]
    held = carry[...]
    held_low = held.astype(BF16)
    state_out[0] = held_low
    from_state = dot(read, held_low)
    low_half = lax.broadcasted_iota(jnp.int32, (1, 128), 1) < 64
    for j in range(pairs):
        lanes = slice(j * 128, (j + 1) * 128)
        x = act[:, lanes]
        xdt = x * spread_heads(step, j, low_half)
        parts = []
        for h in (2 * j, 2 * j + 1):
            decay = jnp.exp(jnp.minimum(cum[:, h : h + 1] - cum_t[h : h + 1, :], 0.0))
            parts.append((decay * inner).astype(BF16))
        xdt_low = xdt.astype(BF16)
        zero = jnp.zeros_like(xdt_low)
        pair = jnp.concatenate([jnp.where(low_half, xdt_low, zero), jnp.where(low_half, zero, xdt_low)], 0)
        y = dot(jnp.concatenate(parts, 1), pair)
        y += spread_heads(enters, j, low_half) * from_state[:, lanes] + chan[0:1, lanes] * x
        scan_out[:, lanes] = y
        fed[:, lanes] = (xdt * spread_heads(to_end, j, low_half)).astype(BF16)
        carry[:, lanes] = held[:, lanes] * spread_heads(keep, j, low_half)
    carry[...] += dot(write_t, fed[...])


def scan_backward_kernel(pre, pre_before, taps, heads, chan, sums, aux, segrow, grad, state, low_out, taps_out, heads_out, ext, gext, act, slope, carry, fed, back, rows):
    n = pre.shape[0]
    pairs = carry.shape[1] // 128
    wide = ext.shape[1]

    @pl.when(pl.program_id(0) == 0)
    def _():
        carry[...] = jnp.zeros_like(carry)
        gext[n:, :] = jnp.zeros((8, wide), F32)
        taps_out[...] = jnp.zeros_like(taps_out)
        heads_out[...] = jnp.zeros_like(heads_out)
        rows[...] = jnp.zeros_like(rows)

    marks = aux[...]
    ext[0:8, :] = pre_before[:, :wide]
    ext[8:, :] = pre[:, :wide]
    for j in range(wide // 128):
        lanes = slice(j * 128, (j + 1) * 128)
        total = conv_strip(ext, taps, marks, j)
        sig = sigmoid(total)
        value = total * sig
        act[:, lanes] = value
        slope[:, lanes] = sig + value * (1.0 - sig)

    step_arg = pre[:, wide:] + heads[0:1, :]
    step = softplus(step_arg)
    rate = heads[1:2, :]
    row = lax.broadcasted_iota(jnp.int32, (n, n), 0)
    col = lax.broadcasted_iota(jnp.int32, (n, n), 1)
    lower = (row >= col).astype(F32)
    cum = jnp.dot(lower, -step * rate, precision=HIGH, preferred_element_type=F32)
    cum_t = cum.T
    write = act[:, pairs * 128 : (pairs + 1) * 128]
    read = act[:, (pairs + 1) * 128 : (pairs + 2) * 128]
    read_t = read.T.astype(BF16)
    write_low = write.astype(BF16)
    read_low = read.astype(BF16)
    allowed = (row <= col) & (marks[:, 8:9] == segrow[0:1, :])
    inner_t = jnp.where(allowed, dot(write_low, read_t), 0.0)
    last = cum[n - 1 : n, :]
    enters = jnp.exp(cum) * marks[:, 3:4]
    to_end = jnp.exp(last - cum) * marks[:, 4:5]
    keep = jnp.exp(last) * marks[n - 1 : n, 3:4]
    held = state[0]
    later = carry[...]
    later_low = later.astype(BF16)
    from_state = dot(read_low, held)
    from_later = dot(write_low, later_low)
    low_half = lax.broadcasted_iota(jnp.int32, (1, 128), 1) < 64
    head_lane = lax.broadcasted_iota(jnp.int32, (1, 128), 1)
    grad_inner = jnp.zeros((n, n), F32)
    col_sums = jnp.zeros((n, 128), F32)
    to_end_part = jnp.zeros((n, 128), F32)
    enter_part = jnp.zeros((n, 128), F32)
    step_part = jnp.zeros((n, 128), F32)
    skip_part = jnp.zeros((n, 128), F32)
    keep_part = jnp.zeros((8, 128), F32)

    def head_sums(value, j):
        high = value.astype(BF16)
        rest = (value - high.astype(F32)).astype(BF16)
        return dot(jnp.concatenate([high, rest], 1), sums[j])

    for j in range(pairs):
        lanes = slice(j * 128, (j + 1) * 128)
        x = act[:, lanes]
        dy = grad[:, lanes].astype(F32)
        step_wide = spread_heads(step, j, low_half)
        xdt = x * step_wide
        xdt_low = xdt.astype(BF16)
        dy_low = dy.astype(BF16)
        zero = jnp.zeros_like(xdt_low)
        products = dot_nt(
            jnp.concatenate([jnp.where(low_half, xdt_low, zero), jnp.where(low_half, zero, xdt_low)], 0),
            dy_low,
        )
        parts = []
        for k, h in enumerate((2 * j, 2 * j + 1)):
            product = products[k * n : (k + 1) * n, :]
            decay = jnp.exp(jnp.minimum(cum_t[h : h + 1, :] - cum[:, h : h + 1], 0.0))
            scaled = decay * product
            grad_inner += scaled
            weighted = scaled * inner_t
            rows[h : h + 1, :] = jnp.sum(weighted, axis=0, keepdims=True)
            col_sums += jnp.where(head_lane == h, jnp.sum(weighted, axis=1, keepdims=True), 0.0)
            parts.append((decay * inner_t).astype(BF16))
        grad_pair = jnp.concatenate([jnp.where(low_half, dy_low, zero), jnp.where(low_half, zero, dy_low)], 0)
        grad_xdt = dot(jnp.concatenate(parts, 1), grad_pair)
        end_wide = spread_heads(to_end, j, low_half)
        enter_wide = spread_heads(enters, j, low_half)
        later_part = end_wide * from_later[:, lanes]
        grad_xdt += later_part
        to_end_part += head_sums(later_part * xdt, j)
        fed[:, lanes] = (xdt * end_wide).astype(BF16)
        grad_enter = dy * enter_wide
        back[:, lanes] = grad_enter.astype(BF16)
        enter_part += head_sums(grad_enter * from_state[:, lanes], j)
        step_part += head_sums(grad_xdt * x, j)
        skip_part += head_sums(dy * x, j)
        kept = jnp.sum(held[:, lanes].astype(F32) * later[:, lanes], axis=0, keepdims=True)
        keep_part += head_sums(jnp.broadcast_to(kept, (8, 128)), j)
        act[:, lanes] = grad_xdt * step_wide + chan[0:1, lanes] * dy
        carry[:, lanes] = later[:, lanes] * spread_heads(keep, j, low_half)

    grad_cum = rows[...].T - col_sums + enter_part - to_end_part
    grad_last = jnp.sum(to_end_part, axis=0, keepdims=True) + keep * keep_part[0:1, :]
    upper = (row <= col).astype(F32)
    grad_log = jnp.dot(upper, grad_cum, precision=HIGH, preferred_element_type=F32) + grad_last
    grad_step = (step_part - rate * grad_log) * sigmoid(step_arg)
    heads_out[0:1, :] += jnp.sum(grad_step, axis=0, keepdims=True)
    heads_out[1:2, :] += -rate * jnp.sum(step * grad_log, axis=0, keepdims=True)
    heads_out[2:3, :] += jnp.sum(skip_part, axis=0, keepdims=True)
    low_out[:, wide:] = grad_step.astype(BF16)

    grad_inner = jnp.where(allowed, grad_inner, 0.0)
    act[:, pairs * 128 : (pairs + 1) * 128] = dot(grad_inner.astype(BF16), read_low) + dot_nt(fed[...], later_low)
    act[:, (pairs + 1) * 128 : (pairs + 2) * 128] = dot(grad_inner.T.astype(BF16), write_low) + dot_nt(back[...], held)
    carry[...] += dot(read_t, back[...])

    for j in range(wide // 128):
        lanes = slice(j * 128, (j + 1) * 128)
        grad_pre = act[:, lanes] * slope[:, lanes]
        gext[0:n, lanes] = grad_pre
        total = taps[3:4, lanes] * grad_pre
        taps_out[3:4, lanes] += jnp.sum(grad_pre * ext[8 : 8 + n, lanes], axis=0, keepdims=True)
        taps_out[4:5, lanes] += jnp.sum(grad_pre, axis=0, keepdims=True)
        for by in (1, 2, 3):
            total += taps[3 - by : 4 - by, lanes] * (marks[:, 4 + by : 5 + by] * gext[by : by + n, lanes])
            taps_out[3 - by : 4 - by, lanes] += jnp.sum(
                grad_pre * (marks[:, by - 1 : by] * ext[8 - by : 8 - by + n, lanes]), axis=0, keepdims=True
            )
        low_out[:, lanes] = total.astype(BF16)
    gext[n:, :] = gext[0:8, :]


def scan_marks(segments):
    length = segments.shape[0]
    blocks = segments.reshape(-1, BLOCK)
    before = jnp.concatenate([jnp.full((1,), -1, jnp.int32), blocks[:-1, -1]], 0)

    def same(by):
        if by > 0:
            other = jnp.concatenate([jnp.full((by,), -1, jnp.int32), segments[:-by]], 0)
        else:
            other = jnp.concatenate([segments[-by:], jnp.full((-by,), -1, jnp.int32)], 0)
        return other == segments

    cols = [same(1), same(2), same(3), (blocks == before[:, None]).reshape(-1), (blocks == blocks[:, -1:]).reshape(-1)]
    cols += [same(-1), same(-2), same(-3), segments]
    marks = jnp.stack([c.astype(F32) for c in cols], 1)
    return jnp.pad(marks, ((0, 0), (0, 128 - len(cols)))), jnp.broadcast_to(segments.astype(F32), (8, length))


def scan_forward(tokens, weights, taps, heads, chan, marks, segrow):
    length, model = tokens.shape
    cols = 1152
    inner = cols - 384
    wide = cols - 128
    n = BLOCK
    blocks = length // n


    return pl.pallas_call(
        scan_forward_kernel,
        grid=(blocks,),
        in_specs=[
            pl.BlockSpec((n, model), lambda i: (i, 0)),
            *first_specs(model),
            whole((8, wide)),
            whole((8, 128)),
            whole((8, inner)),
            pl.BlockSpec((n, 128), lambda i: (i, 0)),
            pl.BlockSpec((8, n), lambda i: (0, i)),
        ],
        out_specs=[
            pl.BlockSpec((n, cols), lambda i: (i, 0)),
            pl.BlockSpec((n, inner), lambda i: (i, 0)),
            pl.BlockSpec((1, 128, inner), lambda i: (i, 0, 0)),
        ],
        out_shape=[
            jax.ShapeDtypeStruct((length, cols), F32),
            jax.ShapeDtypeStruct((length, inner), F32),
            jax.ShapeDtypeStruct((blocks, 128, inner), BF16),
        ],
        scratch_shapes=[
            pltpu.VMEM((n + 8, wide), F32),
            pltpu.VMEM((n, wide), F32),
            pltpu.VMEM((128, inner), F32),
            pltpu.VMEM((n, inner), BF16),
        ],
        compiler_params=PARAMS,
        cost_estimate=cost(20),
        name="scan_forward",
    )(tokens, weights, weights, weights, taps, heads, chan, marks, segrow)


def scan_backward(pre, taps, heads, chan, sums, marks, segrow, grad, states):
    length, cols = pre.shape
    inner = cols - 384
    wide = cols - 128
    n = BLOCK
    blocks = length // n


    def rev(i):
        return blocks - 1 - i

    return pl.pallas_call(
        scan_backward_kernel,
        grid=(blocks,),
        in_specs=[
            pl.BlockSpec((n, cols), lambda i: (rev(i), 0)),
            pl.BlockSpec((8, cols), lambda i: (jnp.maximum(rev(i) * (n // 8) - 1, 0), 0)),
            whole((8, wide)),
            whole((8, 128)),
            whole((8, inner)),
            whole((inner // 128, 256, 128)),
            pl.BlockSpec((n, 128), lambda i: (rev(i), 0)),
            pl.BlockSpec((8, n), lambda i: (0, rev(i))),
            pl.BlockSpec((n, inner), lambda i: (rev(i), 0)),
            pl.BlockSpec((1, 128, inner), lambda i: (rev(i), 0, 0)),
        ],
        out_specs=[
            pl.BlockSpec((n, cols), lambda i: (rev(i), 0)),
            whole((8, wide)),
            whole((8, 128)),
        ],
        out_shape=[
            jax.ShapeDtypeStruct((length, cols), BF16),
            jax.ShapeDtypeStruct((8, wide), F32),
            jax.ShapeDtypeStruct((8, 128), F32),
        ],
        scratch_shapes=[
            pltpu.VMEM((n + 8, wide), F32),
            pltpu.VMEM((n + 8, wide), F32),
            pltpu.VMEM((n, wide), F32),
            pltpu.VMEM((n, wide), F32),
            pltpu.VMEM((128, inner), F32),
            pltpu.VMEM((n, inner), BF16),
            pltpu.VMEM((n, inner), BF16),
            pltpu.VMEM((128, n), F32),
        ],
        compiler_params=PARAMS,
        cost_estimate=cost(30),
        name="scan_backward",
    )(pre, pre, taps, heads, chan, sums, marks, segrow, grad, states)


def head_sum_table(inner):
    pairs = inner // 128
    lane = jnp.arange(256) % 128
    head = 2 * jnp.arange(pairs)[:, None] + (lane >= 64)[None, :]
    return (head[:, :, None] == jnp.arange(128)[None, None, :]).astype(BF16)


def mix_first_kernel(tok, rows, gate_w, out_w, scanned, gain, gate_out, mixed_out, sums_out):
    gate_pre = dot(tok[...], gate_w[...])
    grad_mixed = dot(rows[...], out_w[...])
    gate_out[...] = gate_pre
    mixed_out[...] = grad_mixed
    gated = scanned[...] * (gate_pre * sigmoid(gate_pre))
    square = jnp.sum(gated * gated, axis=1, keepdims=True)
    inner = jnp.sum(grad_mixed * gain[0:1, :] * gated, axis=1, keepdims=True)
    lane = lax.broadcasted_iota(jnp.int32, (1, 128), 1)
    cols = jnp.where(lane == 0, square, jnp.where(lane == 1, inner, 0.0))
    sums_out[...] = cols.T[0:8, :]


def mix_first(tokens, grad_rows, second, scanned, gain):
    length, model = tokens.shape
    width = scanned.shape[1]
    n = 256

    def rows(cols):
        return pl.BlockSpec((n, cols), lambda i: (i, 0))

    return pl.pallas_call(
        mix_first_kernel,
        grid=(length // n,),
        in_specs=[
            rows(model),
            rows(model),
            pl.BlockSpec((model, width), lambda i: (0, 0)),
            pl.BlockSpec((model, width), lambda i: (0, 1)),
            rows(width),
            whole((8, width)),
        ],
        out_specs=[rows(width), rows(width), pl.BlockSpec((8, n), lambda i: (0, i))],
        out_shape=[
            jax.ShapeDtypeStruct((length, width), F32),
            jax.ShapeDtypeStruct((length, width), F32),
            jax.ShapeDtypeStruct((8, length), F32),
        ],
        compiler_params=PARAMS,
        cost_estimate=cost(10),
        name="mix_first",
    )(tokens, grad_rows, second, second, scanned, gain)


def store_block(value, outs):
    for k, out in enumerate(outs):

        @pl.when(pl.program_id(0) == k)
        def _():
            out[...] = value


def mix_second_kernel(channels, me, sums, gate, grad_mixed_in, scanned_in, out_w, gain, low_out, grad_scan, grad_gate, gain_out, *outs):
    n = gate.shape[0]

    @pl.when(pl.program_id(0) == 0)
    def _():
        gain_out[...] = jnp.zeros_like(gain_out)

    cols = jnp.concatenate([sums[...], jnp.zeros((120, n), F32)], 0).T
    scale = lax.rsqrt(cols[:, 0:1] / channels + EPS)
    pull = scale * scale * scale * (cols[:, 1:2] / channels)
    gate_pre = gate[...]
    grad_mixed = grad_mixed_in[...]
    scanned = scanned_in[...]
    sig = sigmoid(gate_pre)
    silu = gate_pre * sig
    gated = scanned * silu
    scaled = gated * scale
    mixed = (scaled * gain[0:1, :]).astype(BF16)
    low_out[...] = mixed
    gain_out[0:1, :] += jnp.sum(grad_mixed * scaled, axis=0, keepdims=True)
    grad_gated = scale * gain[0:1, :] * grad_mixed - gated * pull
    grad_scan[...] = grad_gated * silu
    grad_gate[...] = (grad_gated * scanned * (sig + silu * (1.0 - sig))).astype(BF16)
    store_block(dot_nt(mixed, out_w[...]).astype(BF16), outs)


def mix_second(sums, gate, grad_mixed, scanned, second, gain, channels, spot):
    length, width = gate.shape
    model = second.shape[0]
    n = 256

    def rows(cols):
        return pl.BlockSpec((n, cols), lambda i, me: (me[0] ^ (3 - i), 0))

    return pl.pallas_call(
        lambda *refs: mix_second_kernel(channels, *refs),
        grid_spec=pltpu.PrefetchScalarGridSpec(
            num_scalar_prefetch=1,
            grid=(4,),
            in_specs=[
                pl.BlockSpec((8, n), lambda i, me: (0, me[0] ^ (3 - i))),
                rows(width),
                rows(width),
                rows(width),
                pl.BlockSpec((model, width), lambda i, me: (0, 1)),
                whole((8, width)),
            ],
            out_specs=[rows(width), rows(width), rows(width), whole((8, width))] + [whole((n, model))] * 4,
        ),
        out_shape=[
            jax.ShapeDtypeStruct((length, width), BF16),
            jax.ShapeDtypeStruct((length, width), F32),
            jax.ShapeDtypeStruct((length, width), BF16),
            jax.ShapeDtypeStruct((8, width), F32),
        ]
        + [jax.ShapeDtypeStruct((n, model), BF16)] * 4,
        compiler_params=PARAMS,
        cost_estimate=cost(11),
        name="mix_second",
    )(spot, sums, gate, grad_mixed, scanned, second, gain)


def token_grads_kernel(me, grad_gate, low, gate_w, weights_a, weights_b, weights_c, *outs):
    total = dot_nt(grad_gate[...], gate_w[...])
    for n, w in enumerate((weights_a, weights_b, weights_c)):
        total += dot_nt(low[:, 384 * n : 384 * (n + 1)], w[...])
    store_block(total.astype(BF16), outs)


def token_grads(grad_gate, low, weights, spot, first):
    model = weights.shape[0]
    width = grad_gate.shape[1]
    n = 256

    def rows(cols):
        return pl.BlockSpec((n, cols), lambda i, me: (me[0] ^ (first - i), 0))

    return pl.pallas_call(
        token_grads_kernel,
        grid_spec=pltpu.PrefetchScalarGridSpec(
            num_scalar_prefetch=1,
            grid=(2,),
            in_specs=[rows(width), rows(low.shape[1]), column_block(model, width, 0), *first_specs(model)],
            out_specs=[whole((n, model))] * 2,
        ),
        out_shape=[jax.ShapeDtypeStruct((n, model), BF16)] * 2,
        compiler_params=PARAMS,
        cost_estimate=cost(6),
        name="token_grads",
    )(spot, grad_gate, low, weights, weights, weights, weights)


def row_sums(product):
    sums = jnp.sum(product, axis=1, keepdims=True)
    return jnp.broadcast_to(sums, (product.shape[0], 128)).T[0:1, :]


def second_grads_kernel(tok, rows, grad_gate, mixed, gate_w, out, gains):
    width = grad_gate.shape[1]
    gate_part = lax.dot_general(tok[...], grad_gate[...], TN, preferred_element_type=F32)
    out_part = lax.dot_general(rows[...], mixed[...], TN, preferred_element_type=F32)
    out[:, :width] = gate_part.astype(BF16)
    out[:, width:] = out_part.astype(BF16)
    gains[...] = jnp.broadcast_to(row_sums(gate_part * gate_w[...].astype(F32)), gains.shape)


def second_grads(tokens, grad_rows, grad_gate, mixed, weights):
    length, model = tokens.shape
    width = grad_gate.shape[1]
    n = model // 4
    cols = pl.BlockSpec((length, n), lambda i: (0, i))
    return pl.pallas_call(
        second_grads_kernel,
        grid=(4,),
        in_specs=[cols, cols, whole((length, width)), whole((length, width)), pl.BlockSpec((n, width), lambda i: (i, 0))],
        out_specs=[pl.BlockSpec((n, 2 * width), lambda i: (i, 0)), pl.BlockSpec((8, n), lambda i: (0, i))],
        out_shape=[jax.ShapeDtypeStruct((model, 2 * width), BF16), jax.ShapeDtypeStruct((8, model), F32)],
        compiler_params=PARAMS,
        cost_estimate=cost(8),
        name="second_grads",
    )(tokens, grad_rows, grad_gate, mixed, weights)


def first_grads_kernel(me, tok, low, weights_a, weights_b, weights_c, gate_gains, norm_gain, taps, heads, gain, *rest):
    *outs, packed, gains = rest
    step = pl.program_id(0)
    grad = lax.dot_general(tok[...], low[...], TN, preferred_element_type=F32)
    total = jnp.zeros((grad.shape[0], 128), F32)
    for n, w in enumerate((weights_a, weights_b, weights_c)):
        for m in range(3):
            product = grad[:, 384 * n + 128 * m : 384 * n + 128 * (m + 1)] * w[:, 128 * m : 128 * (m + 1)].astype(F32)
            total += product
    spot = pl.ds(pl.multiple_of(((me[0] + step) % 4) * grad.shape[0], 128), grad.shape[0])
    gains[0:1, spot] = row_sums(total)
    for k in range(4):

        @pl.when(step == k)
        def _():
            outs[k][...] = grad.astype(BF16).reshape(outs[k].shape)

    @pl.when(step == 3)
    def _():
        width = gain.shape[1]
        by_gain = (gains[0:1, :] + gate_gains[0:1, :]) / norm_gain[0:1, :]
        packed[0:5, :] = taps[0:5, :]
        packed[5:6, :width] = gain[0:1, :]
        packed[5:6, width:] = jnp.zeros((1, 1024 - width), F32)
        packed[6:7, :] = by_gain[:, :1024]
        packed[7:8, :512] = by_gain[:, 1024:]
        for r in range(3):
            packed[7:8, 512 + 128 * r : 640 + 128 * r] = heads[r : r + 1, :]
        packed[7:8, 896:] = jnp.zeros((1, 128), F32)


def first_grads(tokens, low, weights, gate_gains, norm_gain, taps, heads, gain, me):
    length, model = tokens.shape
    width = low.shape[1]
    n = model // 4
    shape = (4, n // 4, width)

    def spot(i, me):
        return (me[0] + i) % 4

    return pl.pallas_call(
        first_grads_kernel,
        grid_spec=pltpu.PrefetchScalarGridSpec(
            num_scalar_prefetch=1,
            grid=(4,),
            in_specs=[
                pl.BlockSpec((length, n), lambda i, me: (0, spot(i, me))),
                whole((length, width)),
                pl.BlockSpec((n, 384), lambda i, me: (spot(i, me), 4)),
                pl.BlockSpec((n, 384), lambda i, me: (spot(i, me), 5)),
                pl.BlockSpec((n, 384), lambda i, me: (spot(i, me), 6)),
                whole(gate_gains.shape),
                whole(norm_gain.shape),
                whole(taps.shape),
                whole(heads.shape),
                whole(gain.shape),
            ],
            out_specs=[whole(shape)] * 4 + [whole((8, 1024))],
            scratch_shapes=[pltpu.VMEM((8, model), F32)],
        ),
        out_shape=[jax.ShapeDtypeStruct(shape, BF16)] * 4 + [jax.ShapeDtypeStruct((8, 1024), F32)],
        compiler_params=PARAMS,
        cost_estimate=cost(6),
        name="first_grads",
    )(me, tokens, low, weights, weights, weights, gate_gains, norm_gain, taps, heads, gain)


def add_split_kernel(me, own, ahead, across, behind, *outs):
    for d in range(4):
        e = (me[0] + d) % 4
        total = (own[e].astype(F32) + across[e].astype(F32)) + (ahead[e].astype(F32) + behind[e].astype(F32))
        outs[d][...] = total.astype(BF16)


def add_split(parts, me):
    shape = parts[0].shape[1:]
    return pl.pallas_call(
        add_split_kernel,
        in_specs=[pl.BlockSpec(memory_space=pltpu.SMEM)] + [VMEM_SPEC] * 4,
        out_specs=[VMEM_SPEC] * 4,
        out_shape=[jax.ShapeDtypeStruct(shape, BF16)] * 4,
        compiler_params=PARAMS,
        name="add_split",
    )(me, *parts)


def add_halve_kernel(me, own, ahead, across, behind, keep, give, total):
    total[...] = (own[...].astype(F32) + across[...].astype(F32)) + (ahead[...].astype(F32) + behind[...].astype(F32))
    n = keep.shape[0]
    keep[...] = total[pl.ds(pl.multiple_of(me[0] * n, 16), n), :]
    give[...] = total[pl.ds(pl.multiple_of((1 - me[0]) * n, 16), n), :].astype(BF16)


def add_halve(parts, me):
    rows, width = parts[0].shape
    return pl.pallas_call(
        add_halve_kernel,
        in_specs=[pl.BlockSpec(memory_space=pltpu.SMEM)] + [VMEM_SPEC] * 4,
        out_specs=[VMEM_SPEC] * 2,
        out_shape=[
            jax.ShapeDtypeStruct((rows // 2, width), F32),
            jax.ShapeDtypeStruct((rows // 2, width), BF16),
        ],
        scratch_shapes=[pltpu.VMEM((rows, width), F32)],
        compiler_params=PARAMS,
        name="add_halve",
    )(me, *parts)


def place_kernel(me, *refs):
    out = refs[-1]
    for k, part in enumerate(refs[:-1]):

        @pl.when(pl.program_id(0) == k)
        def _():
            out[...] = part[...].reshape(out.shape)


def place(parts, index, me, shape, block, name):
    return pl.pallas_call(
        place_kernel,
        grid_spec=pltpu.PrefetchScalarGridSpec(
            num_scalar_prefetch=1,
            grid=(len(parts),),
            in_specs=[whole(p.shape) for p in parts],
            out_specs=pl.BlockSpec(block, lambda i, me: index(i, me[0])),
        ),
        out_shape=jax.ShapeDtypeStruct(shape, parts[0].dtype),
        compiler_params=PARAMS,
        cost_estimate=cost(2),
        name=name,
    )(me, *parts)


def shift(value, axis, by):
    n = SIZES[axis]
    return lax.ppermute(value, axis, [(i, (i - by) % n) for i in range(n)])


def swap(value, axis):
    return shift(value, axis, 1)


def ring(value, axis):
    return [value, shift(value, axis, 1), shift(value, axis, 2), shift(value, axis, -1)]


def sends(blocks, axis):
    return [blocks[0], shift(blocks[1], axis, -1), shift(blocks[2], axis, 2), shift(blocks[3], axis, 1)]


def tensor_xor(value, by):
    return lax.ppermute(value, TENSOR, [(i, i ^ by) for i in range(4)])


def sum_ring(value, axis):
    own, ahead, across, behind = ring(value, axis)
    return (own + across) + (ahead + behind)


def sum_pair(value, axis):
    return value + swap(value, axis)


def after(value, *others):
    return lax.optimization_barrier((value,) + others)[0]


def index_of(axis):
    return lax.axis_index(axis).reshape(1).astype(jnp.int32)


def pair_rows(value):
    rows, width = value.shape
    parts = [value, swap(value, "zl")]
    return place(parts, lambda i, me: ((me + i) % 2, 0), index_of("zl"), (2 * rows, width), (rows, width), "place_zl")


def token_place(own, near, far, both, me):
    rows, width = own.shape
    return place([own, near, far, both], lambda i, me: (me ^ i, 0), me, (4 * rows, width), (rows, width), "place_tokens")


def per_device(
    hidden_in,
    norm_gain,
    proj_zx,
    proj_shared,
    proj_step,
    conv_inner,
    conv_shared,
    step_bias,
    decay_log,
    skip_gain,
    gated_gain,
    proj_out,
    out_grad,
    segments,
):
    model_width = hidden_in.shape[1]
    width = proj_zx.shape[2]
    heads = step_bias.shape[0]
    me = {axis: index_of(axis) for axis in DP + TENSOR}
    spot = 2 * me["zh"] + me["c"]

    shared_parts = [proj_shared] + [tensor_xor(proj_shared, by) for by in (1, 2, 3)]
    shared_rows = jnp.zeros((48, 256), BF16)
    for by, part in enumerate(shared_parts):
        shared_rows = lax.dynamic_update_slice(shared_rows, part, (((spot[0] ^ by) * 12), jnp.int32(0)))
    first_rows = jnp.concatenate(
        [proj_zx[:, 1, :], shared_rows, jnp.pad(proj_step, ((0, 0), (0, 128 - heads)))], 1
    )
    all_rows = jnp.concatenate([proj_zx[:, 0, :], proj_out.T, first_rows], 1)
    weights = lax.all_gather(pair_rows(all_rows), ("y", "x"), axis=0, tiled=True)

    residual_in = hidden_in.astype(F32)
    scale_in = lax.rsqrt(jnp.mean(residual_in * residual_in, axis=-1, keepdims=True) + EPS)
    normed_low = (residual_in * scale_in * norm_gain).astype(BF16)
    normed_far = swap(normed_low, "zh")
    normed_near = swap(normed_low, "c")

    normed_both = swap(normed_far, "c")
    tokens = token_place(normed_low, normed_near, normed_far, normed_both, spot)
    grad_far = swap(after(out_grad, normed_far), "zh")
    grad_near = swap(after(out_grad, normed_far), "c")
    grad_both = swap(grad_far, "c")
    grad_rows = token_place(out_grad, grad_near, grad_far, grad_both, spot)

    pad = (0, 128 - heads)
    head_rows = jnp.stack([jnp.pad(step_bias, pad), jnp.pad(jnp.exp(decay_log), pad)], 0)
    head_rows = jnp.pad(head_rows, ((0, 6), (0, 0)))
    taps = jnp.pad(jnp.concatenate([conv_inner, conv_shared], 1), ((0, 3), (0, 0)))
    chan = jnp.broadcast_to(jnp.repeat(skip_gain, width // heads), (8, width))
    gain = jnp.broadcast_to(gated_gain, (8, width))
    norm_rows = jnp.broadcast_to(norm_gain, (8, model_width))
    marks, segrow = scan_marks(segments)
    tokens, grad_rows = lax.optimization_barrier((tokens, grad_rows))
    pre, scanned, states = scan_forward(tokens, weights, taps, head_rows, chan, marks, segrow)

    gate_pre, grad_mixed, sums = mix_first(tokens, grad_rows, weights, scanned, gain)
    sums = (sums + tensor_xor(sums, 1)) + (tensor_xor(sums, 2) + tensor_xor(sums, 3))
    mixed_low, grad_scanned, gate_grad_low, gain_sums, *out_blocks = mix_second(
        sums, gate_pre, grad_mixed, scanned, weights, gain, 4 * width, spot
    )
    out_far = (out_blocks[1].astype(F32) + swap(out_blocks[0], "c").astype(F32)).astype(BF16)
    out_near = swap(out_blocks[2], "c")
    second_total, gate_gains = second_grads(tokens, grad_rows, gate_grad_low, mixed_low, weights)
    second_sum = lax.psum_scatter(second_total, ("y", "x"), scatter_dimension=0, tiled=True)
    out_far_got = swap(out_far, "zh")

    sum_table = head_sum_table(width)
    grad_scanned = after(grad_scanned, out_far, second_total)
    low, tap_sums, head_sums = scan_backward(
        pre, taps, head_rows, chan, sum_table, marks, segrow, grad_scanned, states
    )
    low = after(low, out_far_got)
    *first_blocks, small = first_grads(
        tokens, low, weights, gate_gains, norm_rows, tap_sums, head_sums, gain_sums, me["y"]
    )
    first_parts = sends(first_blocks, "y")
    low_late = after(low, *first_blocks)
    far_give, far_keep = token_grads(gate_grad_low, low_late, weights, spot, 3)
    far_got = jnp.concatenate([swap(far_give[:128], "c"), swap(far_give[128:], "c")], 0)
    near_give, near_keep = token_grads(gate_grad_low, after(low_late, far_give), weights, spot, 1)
    near_got = swap(near_give, "c")
    row_far = (far_keep.astype(F32) + far_got.astype(F32)).astype(BF16)
    row_far_got = swap(row_far, "zh")

    first_parts = [after(part, row_far_got, near_give) for part in first_parts]
    first_halves = add_split(first_parts, me["x"])
    first_parts = sends(first_halves, "x")
    small = sum_ring(after(small, *first_halves), "y")
    first_keep, first_give = add_halve(first_parts, me["zl"])
    small = sum_ring(after(small, first_give), "x")
    small = sum_pair(small, "zl")
    first_mine = first_keep + swap(first_give, "zl").astype(F32)
    second_pairs = second_sum.reshape(2, 48, 2 * width)
    second_keep = lax.dynamic_index_in_dim(second_pairs, me["zl"][0], 0, keepdims=False)
    second_mine = second_keep.astype(F32) + swap(
        lax.dynamic_index_in_dim(second_pairs, 1 - me["zl"][0], 0, keepdims=False), "zl"
    ).astype(F32)

    hidden_out = (
        residual_in + (out_blocks[3].astype(F32) + out_near.astype(F32) + out_far_got.astype(F32))
    ).astype(BF16)
    grad_normed = near_keep.astype(F32) + near_got.astype(F32) + row_far_got.astype(F32)
    weighted = jnp.sum(grad_normed * norm_gain * residual_in, axis=-1, keepdims=True)
    grad_hidden = (
        out_grad.astype(F32)
        + scale_in * norm_gain * grad_normed
        - residual_in * scale_in**3 * weighted / model_width
    ).astype(BF16)
    grad_proj_out = second_mine[:, width:].T
    grad_proj_zx = jnp.stack([second_mine[:, :width], first_mine[:, :width]], 1)
    grad_proj_step = first_mine[:, width + 256 : width + 256 + heads]

    def quarter(by):
        return lax.dynamic_slice(first_mine, ((spot[0] ^ by) * 12, jnp.int32(width)), (12, 256))

    grad_proj_shared = (quarter(0) + tensor_xor(quarter(1), 1)) + (
        tensor_xor(quarter(2), 2) + tensor_xor(quarter(3), 3)
    )

    summed = (small + tensor_xor(small, 1)) + (tensor_xor(small, 2) + tensor_xor(small, 3))
    grad_norm_gain = jnp.concatenate([summed[6], summed[7, :512]])
    return (
        hidden_out,
        grad_hidden,
        grad_norm_gain,
        grad_proj_zx,
        grad_proj_shared,
        grad_proj_step,
        small[:5, :width],
        summed[:5, width:],
        small[7, 512 : 512 + heads],
        small[7, 640 : 640 + heads],
        small[7, 768 : 768 + heads],
        small[5, :width],
        grad_proj_out,
    )


def solution(mesh):
    fine = Mesh(mesh.devices.reshape(4, 4, 2, 2, 2), DP + TENSOR)
    both = DP + TENSOR
    return jax.shard_map(
        per_device,
        mesh=fine,
        in_specs=(
            P(both, None),
            P(),
            P(DP, None, TENSOR),
            P(both, None),
            P(DP, TENSOR),
            P(None, TENSOR),
            P(),
            P(TENSOR),
            P(TENSOR),
            P(TENSOR),
            P(TENSOR),
            P(TENSOR, DP),
            P(both, None),
            P(DP),
        ),
        out_specs=(
            P(both, None),
            P(both, None),
            P(),
            P(DP, None, TENSOR),
            P(both, None),
            P(DP, TENSOR),
            P(None, TENSOR),
            P(),
            P(TENSOR),
            P(TENSOR),
            P(TENSOR),
            P(TENSOR),
            P(TENSOR, DP),
        ),
        check_vma=False,
    )
```

profile of v0, /device:TPU:24, one launch (start us, length us, event | category | flops | bytes accessed | tf_op | source)
XLA Modules:
  0.0 335.8 jit_solution(11303768348352732858)
XLA Ops:
  7.3 4.0 %collective-permute-start.7 = (bf16[12,256]{1,0:T(8,128)(2,1)}, bf16[12,256]{1,0:T(8,128)(2,1)S(1)}, u32[]{:S(2)}, u32[]{:S(2)}) collective-permute-start(bf16[12,256]{1,0:T(8,128)(2,1)} %param.17), channel_id=1, source_target_pairs={{0,2},{1,3},{2,0},{3,1},{4,6},{5,7},{6,4},{7,5},{8,10},{9,11},{10,... | collective-permute-start | bytes 18440 | tf_op jit(solution)/shard_map/ppermute | solution.py:713
  17.3 7.3 %collective-permute-done.9.refs_1_ = bf16[48,2688]{1,0:T(8,128)(2,1)S(1)} collective-permute-done((bf16[48,2688]{1,0:T(8,128)(2,1)S(1)}, bf16[48,2688]{1,0:T(8,128)(2,1)S(1)}, u32[]{:S(2)}, u32[]{:S(2)}) %collective-permute-start.9) | collective-permute-done | bytes 258080 | tf_op jit(solution)/shard_map/ppermute | solution.py:697
  27.8 3.2 collective-permute-start.1
  31.0 17.4 %collective-permute-done.1.refs_2_ = bf16[256,1536]{1,0:T(8,128)(2,1)} collective-permute-done((bf16[256,1536]{1,0:T(8,128)(2,1)S(1)}, bf16[256,1536]{1,0:T(8,128)(2,1)}, u32[]{:S(2)}, u32[]{:S(2)}) %collective-permute-start.1) | collective-permute-done | bytes 786464 | tf_op jit(solution)/shard_map/ppermute | solution.py:697
  48.3 3.2 collective-permute-start.4
  52.7 15.3 %collective-permute-done.4.refs_2_ = bf16[256,1536]{1,0:T(8,128)(2,1)} collective-permute-done((bf16[256,1536]{1,0:T(8,128)(2,1)S(1)}, bf16[256,1536]{1,0:T(8,128)(2,1)}, u32[]{:S(2)}, u32[]{:S(2)}) %collective-permute-start.4) | collective-permute-done | bytes 786464 | tf_op jit(solution)/shard_map/ppermute | solution.py:697
  70.8 4.1 %place_tokens.2.tok = bf16[1024,1536]{1,0:T(8,128)(2,1)} custom-call(s32[1]{0:T(128)} %bitcast.me.refs_0_, bf16[256,1536]{1,0:T(8,128)(2,1)} %copy-done.1, bf16[256,1536]{1,0:T(8,128)(2,1)} %collective-permute-done.refs_1_, bf16[256,1536]{1,0:T(8,128)(2,1)} %collective-permute-done.1.refs_2_, bf16[256,1536]{1,0:T(8,128)(2,1)} %collective-permute-done.2.refs_3_), custom_call_target="tpu_custom_call" | custom-call | flops 2000000 | bytes 6000 | tf_op jit(solution)/shard_map/place_tokens/pallas_call | solution.py:680
  74.8 4.2 %place_tokens.3.rows = bf16[1024,1536]{1,0:T(8,128)(2,1)} custom-call(s32[1]{0:T(128)} %bitcast.me.refs_0_, bf16[256,1536]{1,0:T(8,128)(2,1)} %refs_0_.1, bf16[256,1536]{1,0:T(8,128)(2,1)} %collective-permute-done.3.refs_1_, bf16[256,1536]{1,0:T(8,128)(2,1)} %collective-permute-done.4.refs_2_, bf16[256,1536]{1,0:T(8,128)(2,1)} %collective-permute-done.5.refs_3_), custom_call_target="tpu_custom_call" | custom-call | flops 2000000 | bytes 6000 | tf_op jit(solution)/shard_map/place_tokens/pallas_call | solution.py:680
  79.1 19.5 %all-gather.2.cloned.1.call-done.weights_a.weights_b.weights_c.gate_w.out_w.refs_5_ = bf16[1536,2688]{1,0:T(8,128)(2,1)} async-done(((bf16[96,2688]{1,0:T(8,128)(2,1)}), bf16[1536,2688]{1,0:T(8,128)(2,1)}) %all-gather.2.cloned.1.call-update) | async-done | bytes 8257552 | tf_op jit(solution)/shard_map/all_gather | solution.py:774
  99.8 20.8 %scan_forward.1 = (f32[1024,1152]{1,0:T(8,128)}, f32[1024,768]{1,0:T(8,128)}, bf16[8,128,768]{2,1,0:T(8,128)(2,1)}) custom-call(bf16[1024,1536]{1,0:T(8,128)(2,1)} %place_tokens.2.tok, bf16[1536,2688]{1,0:T(8,128)(2,1)} %all-gather.2.cloned.1.call-done.weights_a.weights_b.weights_c.gate_w.out_w.refs_5_, ...), custom_call_target="tpu_custom_call" | custom-call | flops 20000000 | bytes 60000 | tf_op jit(solution)/shard_map/scan_forward/pallas_call | solution.py:293
  121.2 10.6 %mix_first.1 = (f32[1024,768]{1,0:T(8,128)}, f32[1024,768]{1,0:T(8,128)}, f32[8,1024]{1,0:T(8,128)}) custom-call(bf16[1024,1536]{1,0:T(8,128)(2,1)} %place_tokens.2.tok, bf16[1024,1536]{1,0:T(8,128)(2,1)} %place_tokens.3.rows, bf16[1536,2688]{1,0:T(8,128)(2,1)} %all-gather.2.cloned.1.call-done.weights_a.weights_b.weights_c.gate_w.out_w.refs_5_, ...), custom_call_target="tpu_custom_call" | custom-call | flops 10000000 | bytes 30000 | tf_op jit(solution)/shard_map/mix_first/pallas_call | solution.py:407
  131.8 3.3 collective-permute-start.11
  135.2 2.3 collective-permute-done.11
  137.5 2.6 collective-permute-done.12
  141.5 11.7 %mix_second.1 = (bf16[1024,768]{1,0:T(8,128)(2,1)}, f32[1024,768]{1,0:T(8,128)}, bf16[1024,768]{1,0:T(8,128)(2,1)}, f32[8,768]{1,0:T(8,128)}, bf16[256,1536]{1,0...) custom-call(s32[1]{0:T(128)} %bitcast.me.refs_0_, ...), custom_call_target="tpu_custom_call" | custom-call | flops 11000000 | bytes 33000 | tf_op jit(solution)/shard_map/mix_second/pallas_call | solution.py:472
  153.2 10.3 %second_grads.1 = (bf16[1536,1536]{1,0:T(8,128)(2,1)}, f32[8,1536]{1,0:T(8,128)}) custom-call(bf16[1024,1536]{1,0:T(8,128)(2,1)} %place_tokens.2.tok, bf16[1024,1536]{1,0:T(8,128)(2,1)} %place_tokens.3.rows, bf16[1024,768]{1,0:T(8,128)(2,1)} %get-tuple-element.71.grad_gate, bf16[1024,768]{1,0:T(8,128)(2,1)} %get-tuple-element.74.mixed, ...), custom_call_target="tpu_custom_call" | custom-call | flops 8000000 | bytes 24000 | tf_op jit(solution)/shard_map/second_grads/pallas_call | solution.py:549
  169.0 30.4 %scan_backward.1 = (bf16[1024,1152]{1,0:T(8,128)(2,1)}, f32[8,1024]{1,0:T(8,128)}, f32[8,128]{1,0:T(8,128)}) custom-call(f32[1024,1152]{1,0:T(8,128)} %get-tuple-element.72.pre.pre_before, f32[1024,1152]{1,0:T(8,128)} %get-tuple-element.72.pre.pre_before, f32[8,1024]{1,0:T(8,128)} %select_maximum_fusion.taps, f32[8,128]{1,0:T(8,128)} %select_maximum_fusion.1.heads, ...), custom_call_target="tpu_custom_call" | custom-call | flops 30000000 | bytes 90000 | tf_op jit(solution)/shard_map/scan_backward/pallas_call | solution.py:338
  200.1 10.3 %first_grads.1 = (bf16[4,96,1152]{2,1,0:T(8,128)(2,1)}, bf16[4,96,1152]{2,1,0:T(8,128)(2,1)}, bf16[4,96,1152]{2,1,0:T(8,128)(2,1)}, bf16[4,96,1152]{2,1,0:T(8,128)(2,1)}, f32[8,1024]{1,0:T(8,128)}) custom-call(s32[1]{0:T(128)} %bitcast.23.me, bf16[1024,1536]{1,0:T(8,128)(2,1)} %place_tokens.2.tok, bf16[1024,1152]{1,0:T(8,128)(2,1)} %get-tuple-element.90.low, ...), custom_call_target="tpu_custom_call" | custom-call | flops 6000000 | bytes 18000 | tf_op jit(solution)/shard_map/first_grads/pallas_call | solution.py:601
  210.4 8.5 %token_grads.2 = (bf16[256,1536]{1,0:T(8,128)(2,1)}, bf16[256,1536]{1,0:T(8,128)(2,1)}) custom-call(s32[1]{0:T(128)} %bitcast.me.refs_0_, bf16[1024,768]{1,0:T(8,128)(2,1)} %get-tuple-element.71.grad_gate, bf16[1024,1152]{1,0:T(8,128)(2,1)} %get-tuple-element.90.low, ...), custom_call_target="tpu_custom_call" | custom-call | flops 6000000 | bytes 18000 | tf_op jit(solution)/shard_map/token_grads/pallas_call | solution.py:515
  224.9 3.1 collective-permute-start.19
  228.0 8.4 %token_grads.3 = (bf16[256,1536]{1,0:T(8,128)(2,1)}, bf16[256,1536]{1,0:T(8,128)(2,1)}) custom-call(s32[1]{0:T(128)} %bitcast.me.refs_0_, bf16[1024,768]{1,0:T(8,128)(2,1)} %get-tuple-element.71.grad_gate, bf16[1024,1152]{1,0:T(8,128)(2,1)} %get-tuple-element.90.low, ...), custom_call_target="tpu_custom_call" | custom-call | flops 6000000 | bytes 18000 | tf_op jit(solution)/shard_map/token_grads/pallas_call | solution.py:515
  236.4 17.9 %collective-permute-done.22.behind = bf16[4,96,1152]{2,1,0:T(8,128)(2,1)} collective-permute-done((bf16[4,96,1152]{2,1,0:T(8,128)(2,1)S(1)}, bf16[4,96,1152]{2,1,0:T(8,128)(2,1)}, u32[]{:S(2)}, u32[]{:S(2)}) %collective-permute-start.22) | collective-permute-done | bytes 884768 | tf_op jit(solution)/shard_map/ppermute | solution.py:697
  254.3 11.9 %collective-permute-done.21.across = bf16[4,96,1152]{2,1,0:T(8,128)(2,1)} collective-permute-done((bf16[4,96,1152]{2,1,0:T(8,128)(2,1)}, bf16[4,96,1152]{2,1,0:T(8,128)(2,1)}, u32[]{:S(2)}, u32[]{:S(2)}) %collective-permute-start.21) | collective-permute-done | bytes 884768 | tf_op jit(solution)/shard_map/ppermute | solution.py:697
  268.2 3.2 add_split.1
  272.7 2.1 collective-permute-start.24
  280.9 7.2 %collective-permute-done.26.ahead = bf16[96,1152]{1,0:T(8,128)(2,1)S(1)} collective-permute-done((bf16[96,1152]{1,0:T(8,128)(2,1)}, bf16[96,1152]{1,0:T(8,128)(2,1)S(1)}, u32[]{:S(2)}, u32[]{:S(2)}) %collective-permute-start.26) | collective-permute-done | bytes 221216 | tf_op jit(solution)/shard_map/ppermute | solution.py:697
  289.6 2.2 add_halve.1
  297.4 2.9 collective-permute-done.31
  301.6 3.4 %fusion.7 = (bf16[256,1536]{1,0:T(8,128)(2,1)}, bf16[256,1536]{1,0:T(8,128)(2,1)}) fusion(bf16[256,1536]{1,0:T(8,128)(2,1)S(1)} %copy-done, bf16[256,1536]{1,0:T(8,128)(2,1)S(1)} %copy-done.3, bf16[256,1536]{1,0:T(8,128)(2,1)S(1)} %collective-permute-done.19, bf16[256,1536]{1,0:T(8,128)(2,1)S(1)} %collective-permute-done.16, ...), kind=kLoop, calls=%fused_computation.12 | loop fusion | flops 8650752 | bytes 7873536 | tf_op jit(solution)/shard_map/convert_element_type | solution.py:852
  306.0 2.9 collective-permute-start.34
  316.3 2.2 collective-permute-start.40
  321.6 4.8 %collective-permute-done.36 = bf16[48,1536]{1,0:T(8,128)(2,1)S(1)} collective-permute-done((bf16[48,1536]{1,0:T(8,128)(2,1)S(1)}, bf16[48,1536]{1,0:T(8,128)(2,1)S(1)}, u32[]{:S(2)}, u32[]{:S(2)}) %collective-permute-start.36) | collective-permute-done | bytes 147488 | tf_op jit(solution)/shard_map/ppermute | solution.py:697
  (193 shorter events, 60.3 us)
Async XLA Ops:
  7.2 91.4 %all-gather.2.cloned.1.call-start = ((), (), s32[]{:S(2)}) async-start(), calls=%async_computation.1 | async-start | bytes 8773632 | tf_op jit(solution)/shard_map/all_gather | solution.py:774
  7.2 8.0 %collective-permute-start.6 = (bf16[12,256]{1,0:T(8,128)(2,1)}, bf16[12,256]{1,0:T(8,128)(2,1)S(1)}, u32[]{:S(2)}, u32[]{:S(2)}) collective-permute-start(bf16[12,256]{1,0:T(8,128)(2,1)} %param.17), channel_id=1, source_target_pairs={{0,1},{1,0},{2,3},{3,2},{4,5},{5,4},{6,7},{7,6},{8,9},{9,8},{10,11... | collective-permute-start | bytes 18440 | tf_op jit(solution)/shard_map/ppermute | solution.py:713
  7.3 8.1 %collective-permute-start.7 = (bf16[12,256]{1,0:T(8,128)(2,1)}, bf16[12,256]{1,0:T(8,128)(2,1)S(1)}, u32[]{:S(2)}, u32[]{:S(2)}) collective-permute-start(bf16[12,256]{1,0:T(8,128)(2,1)} %param.17), channel_id=1, source_target_pairs={{0,2},{1,3},{2,0},{3,1},{4,6},{5,7},{6,4},{7,5},{8,10},{9,11},{10,... | collective-permute-start | bytes 18440 | tf_op jit(solution)/shard_map/ppermute | solution.py:713
  16.2 8.4 %collective-permute-start.9 = (bf16[48,2688]{1,0:T(8,128)(2,1)S(1)}, bf16[48,2688]{1,0:T(8,128)(2,1)S(1)}, u32[]{:S(2)}, u32[]{:S(2)}) collective-permute-start(bf16[48,2688]{1,0:T(8,128)(2,1)S(1)} %pad_dynamic-update-slice_fusion.refs_0_), channel_id=1, source_target_pairs={{0,4},{4,0},{1,5},{5,1},{2,6},{6,2},{3,7},{7,3},{8,12},{12,8},{9,1... | collective-permute-start | bytes 774152 | tf_op jit(solution)/shard_map/ppermute | solution.py:697
  27.2 292.0 %reduce-scatter.2.cloned.1.call-start = ((), (), s32[]{:S(2)}) async-start(), calls=%async_computation.2 | async-start | bytes 5013504 | tf_op jit(solution)/shard_map/reduce_scatter | solution.py:808
  27.8 20.5 %collective-permute-start.1 = (bf16[256,1536]{1,0:T(8,128)(2,1)S(1)}, bf16[256,1536]{1,0:T(8,128)(2,1)}, u32[]{:S(2)}, u32[]{:S(2)}) collective-permute-start(bf16[256,1536]{1,0:T(8,128)(2,1)S(1)} %fusion.2.refs_0_), channel_id=1, source_target_pairs={{0,2},{2,0},{1,3},{3,1},{4,6},{6,4},{5,7},{7,5},{8,10},{10,8},{9,1... | collective-permute-start | bytes 2359304 | tf_op jit(solution)/shard_map/ppermute | solution.py:697
  48.3 19.7 %collective-permute-start.4 = (bf16[256,1536]{1,0:T(8,128)(2,1)S(1)}, bf16[256,1536]{1,0:T(8,128)(2,1)}, u32[]{:S(2)}, u32[]{:S(2)}) collective-permute-start(bf16[256,1536]{1,0:T(8,128)(2,1)S(1)} %copy-done.2), channel_id=1, source_target_pairs={{0,2},{2,0},{1,3},{3,1},{4,6},{6,4},{5,7},{7,5},{8,10},{10,8},{9,1... | collective-permute-start | bytes 2359304 | tf_op jit(solution)/shard_map/ppermute | solution.py:697
  51.6 19.2 %collective-permute-start = (bf16[256,1536]{1,0:T(8,128)(2,1)S(1)}, bf16[256,1536]{1,0:T(8,128)(2,1)}, u32[]{:S(2)}, u32[]{:S(2)}) collective-permute-start(bf16[256,1536]{1,0:T(8,128)(2,1)S(1)} %fusion.2.refs_0_), channel_id=1, source_target_pairs={{0,1},{1,0},{2,3},{3,2},{4,5},{5,4},{6,7},{7,6},{8,9},{9,8},{10,11... | collective-permute-start | bytes 2359304 | tf_op jit(solution)/shard_map/ppermute | solution.py:697
  52.2 22.7 %collective-permute-start.3 = (bf16[256,1536]{1,0:T(8,128)(2,1)S(1)}, bf16[256,1536]{1,0:T(8,128)(2,1)}, u32[]{:S(2)}, u32[]{:S(2)}) collective-permute-start(bf16[256,1536]{1,0:T(8,128)(2,1)S(1)} %copy-done.2), channel_id=1, source_target_pairs={{0,1},{1,0},{2,3},{3,2},{4,5},{5,4},{6,7},{7,6},{8,9},{9,8},{10,11... | collective-permute-start | bytes 2359304 | tf_op jit(solution)/shard_map/ppermute | solution.py:697
  52.7 18.1 %collective-permute-start.2 = (bf16[256,1536]{1,0:T(8,128)(2,1)}, bf16[256,1536]{1,0:T(8,128)(2,1)}, u32[]{:S(2)}, u32[]{:S(2)}) collective-permute-start(bf16[256,1536]{1,0:T(8,128)(2,1)} %collective-permute-done.1.refs_2_), channel_id=1, source_target_pairs={{0,1},{1,0},{2,3},{3,2},{4,5},{5,4},{6,7},{7,6},{8,9},{9,8},{10,11... | collective-permute-start | bytes 2359304 | tf_op jit(solution)/shard_map/ppermute | solution.py:697
  68.0 6.8 %collective-permute-start.5 = (bf16[256,1536]{1,0:T(8,128)(2,1)}, bf16[256,1536]{1,0:T(8,128)(2,1)}, u32[]{:S(2)}, u32[]{:S(2)}) collective-permute-start(bf16[256,1536]{1,0:T(8,128)(2,1)} %collective-permute-done.4.refs_2_), channel_id=1, source_target_pairs={{0,1},{1,0},{2,3},{3,2},{4,5},{5,4},{6,7},{7,6},{8,9},{9,8},{10,11... | collective-permute-start | bytes 2359304 | tf_op jit(solution)/shard_map/ppermute | solution.py:697
  131.8 5.7 %collective-permute-start.11 = (f32[8,1024]{1,0:T(8,128)}, f32[8,1024]{1,0:T(8,128)S(1)}, u32[]{:S(2)}, u32[]{:S(2)}) collective-permute-start(f32[8,1024]{1,0:T(8,128)} %get-tuple-element.64), channel_id=1, source_target_pairs={{0,2},{1,3},{2,0},{3,1},{4,6},{5,7},{6,4},{7,5},{8,10},{9,11},{10,... | collective-permute-start | bytes 98312 | tf_op jit(solution)/shard_map/ppermute | solution.py:713
  167.1 32.3 %collective-permute-start.15 = (bf16[256,1536]{1,0:T(8,128)(2,1)S(1)}, bf16[256,1536]{1,0:T(8,128)(2,1)S(1)}, u32[]{:S(2)}, u32[]{:S(2)}) collective-permute-start(bf16[256,1536]{1,0:T(8,128)(2,1)S(1)} %add_convert_fusion.1), channel_id=1, source_target_pairs={{0,2},{2,0},{1,3},{3,1},{4,6},{6,4},{5,7},{7,5},{8,10},{10,8},{9,1... | collective-permute-start | bytes 2359304 | tf_op jit(solution)/shard_map/ppermute | solution.py:697
  220.7 33.6 %collective-permute-start.22 = (bf16[4,96,1152]{2,1,0:T(8,128)(2,1)S(1)}, bf16[4,96,1152]{2,1,0:T(8,128)(2,1)}, u32[]{:S(2)}, u32[]{:S(2)}) collective-permute-start(bf16[4,96,1152]{2,1,0:T(8,128)(2,1)S(1)} %copy-done.24), channel_id=1, source_target_pairs={{0,96},{32,0},{64,32},{96,64},{1,97},{33,1},{65,33},{97,65},{2,98}... | collective-permute-start | bytes 2654216 | tf_op jit(solution)/shard_map/ppermute | solution.py:697
  221.5 44.7 %collective-permute-start.21 = (bf16[4,96,1152]{2,1,0:T(8,128)(2,1)}, bf16[4,96,1152]{2,1,0:T(8,128)(2,1)}, u32[]{:S(2)}, u32[]{:S(2)}) collective-permute-start(bf16[4,96,1152]{2,1,0:T(8,128)(2,1)} %get-tuple-element.86), channel_id=1, source_target_pairs={{0,64},{32,96},{64,0},{96,32},{1,65},{33,97},{65,1},{97,33},{2,66}... | collective-permute-start | bytes 2654216 | tf_op jit(solution)/shard_map/ppermute | solution.py:697
  222.7 45.5 %collective-permute-start.20 = (bf16[4,96,1152]{2,1,0:T(8,128)(2,1)}, bf16[4,96,1152]{2,1,0:T(8,128)(2,1)}, u32[]{:S(2)}, u32[]{:S(2)}) collective-permute-start(bf16[4,96,1152]{2,1,0:T(8,128)(2,1)} %get-tuple-element.85), channel_id=1, source_target_pairs={{0,32},{32,64},{64,96},{96,0},{1,33},{33,65},{65,97},{97,1},{2,34}... | collective-permute-start | bytes 2654216 | tf_op jit(solution)/shard_map/ppermute | solution.py:697
  224.9 29.4 %collective-permute-start.19 = (bf16[256,1536]{1,0:T(8,128)(2,1)S(1)}, bf16[256,1536]{1,0:T(8,128)(2,1)S(1)}, u32[]{:S(2)}, u32[]{:S(2)}) collective-permute-start(bf16[256,1536]{1,0:T(8,128)(2,1)S(1)} %add_convert_fusion), channel_id=1, source_target_pairs={{0,2},{2,0},{1,3},{3,1},{4,6},{6,4},{5,7},{7,5},{8,10},{10,8},{9,1... | collective-permute-start | bytes 2359304 | tf_op jit(solution)/shard_map/ppermute | solution.py:697
  236.4 58.7 %collective-permute-start.16 = (bf16[256,1536]{1,0:T(8,128)(2,1)}, bf16[256,1536]{1,0:T(8,128)(2,1)S(1)}, u32[]{:S(2)}, u32[]{:S(2)}) collective-permute-start(bf16[256,1536]{1,0:T(8,128)(2,1)} %get-tuple-element.92), channel_id=1, source_target_pairs={{0,1},{1,0},{2,3},{3,2},{4,5},{5,4},{6,7},{7,6},{8,9},{9,8},{10,11... | collective-permute-start | bytes 2359304 | tf_op jit(solution)/shard_map/ppermute | solution.py:697
  254.3 47.2 %collective-permute-start.13 = (bf16[256,1536]{1,0:T(8,128)(2,1)}, bf16[256,1536]{1,0:T(8,128)(2,1)}, u32[]{:S(2)}, u32[]{:S(2)}) collective-permute-start(bf16[256,1536]{1,0:T(8,128)(2,1)} %get-tuple-element.68), channel_id=1, source_target_pairs={{0,1},{1,0},{2,3},{3,2},{4,5},{5,4},{6,7},{7,6},{8,9},{9,8},{10,11... | collective-permute-start | bytes 2359304 | tf_op jit(solution)/shard_map/ppermute | solution.py:697
  271.3 5.6 %collective-permute-start.23 = (f32[8,1024]{1,0:T(8,128)S(1)}, f32[8,1024]{1,0:T(8,128)S(1)}, u32[]{:S(2)}, u32[]{:S(2)}) collective-permute-start(f32[8,1024]{1,0:T(8,128)S(1)} %copy-done.18), channel_id=1, source_target_pairs={{0,64},{32,96},{64,0},{96,32},{1,65},{33,97},{65,1},{97,33},{2,66}... | collective-permute-start | bytes 98312 | tf_op jit(solution)/shard_map/ppermute | solution.py:697
  277.0 11.2 %collective-permute-start.26 = (bf16[96,1152]{1,0:T(8,128)(2,1)}, bf16[96,1152]{1,0:T(8,128)(2,1)S(1)}, u32[]{:S(2)}, u32[]{:S(2)}) collective-permute-start(bf16[96,1152]{1,0:T(8,128)(2,1)} %get-tuple-element.100), channel_id=1, source_target_pairs={{0,8},{8,16},{16,24},{24,0},{1,9},{9,17},{17,25},{25,1},{2,10},{10... | collective-permute-start | bytes 663560 | tf_op jit(solution)/shard_map/ppermute | solution.py:697
  277.8 10.3 %collective-permute-start.27 = (bf16[96,1152]{1,0:T(8,128)(2,1)}, bf16[96,1152]{1,0:T(8,128)(2,1)S(1)}, u32[]{:S(2)}, u32[]{:S(2)}) collective-permute-start(bf16[96,1152]{1,0:T(8,128)(2,1)} %get-tuple-element.101), channel_id=1, source_target_pairs={{0,16},{8,24},{16,0},{24,8},{1,17},{9,25},{17,1},{25,9},{2,18},{10... | collective-permute-start | bytes 663560 | tf_op jit(solution)/shard_map/ppermute | solution.py:697
  279.6 9.2 %collective-permute-start.28 = (bf16[96,1152]{1,0:T(8,128)(2,1)}, bf16[96,1152]{1,0:T(8,128)(2,1)S(1)}, u32[]{:S(2)}, u32[]{:S(2)}) collective-permute-start(bf16[96,1152]{1,0:T(8,128)(2,1)} %get-tuple-element.102), channel_id=1, source_target_pairs={{0,24},{8,0},{16,8},{24,16},{1,25},{9,1},{17,9},{25,17},{2,26},{10... | collective-permute-start | bytes 663560 | tf_op jit(solution)/shard_map/ppermute | solution.py:697
  291.8 5.5 %collective-permute-start.29 = (f32[8,1024]{1,0:T(8,128)S(1)}, f32[8,1024]{1,0:T(8,128)S(1)}, u32[]{:S(2)}, u32[]{:S(2)}) collective-permute-start(f32[8,1024]{1,0:T(8,128)S(1)} %add_add_fusion.2), channel_id=1, source_target_pairs={{0,16},{8,24},{16,0},{24,8},{1,17},{9,25},{17,1},{25,9},{2,18},{10... | collective-permute-start | bytes 98312 | tf_op jit(solution)/shard_map/ppermute | solution.py:697
  295.1 5.1 %collective-permute-start.31 = (f32[8,1024]{1,0:T(8,128)S(1)}, f32[8,1024]{1,0:T(8,128)S(1)}, u32[]{:S(2)}, u32[]{:S(2)}) collective-permute-start(f32[8,1024]{1,0:T(8,128)S(1)} %add_add_fusion.2), channel_id=1, source_target_pairs={{0,8},{8,16},{16,24},{24,0},{1,9},{9,17},{17,25},{25,1},{2,10},{10... | collective-permute-start | bytes 98312 | tf_op jit(solution)/shard_map/ppermute | solution.py:697
  300.3 5.6 %collective-permute-start.32 = (f32[8,1024]{1,0:T(8,128)S(1)}, f32[8,1024]{1,0:T(8,128)S(1)}, u32[]{:S(2)}, u32[]{:S(2)}) collective-permute-start(f32[8,1024]{1,0:T(8,128)S(1)} %add_add_fusion.1), channel_id=1, source_target_pairs={{0,4},{4,0},{1,5},{5,1},{2,6},{6,2},{3,7},{7,3},{8,12},{12,8},{9,1... | collective-permute-start | bytes 98312 | tf_op jit(solution)/shard_map/ppermute | solution.py:697
  305.0 9.9 %collective-permute-start.37 = (bf16[48,1152]{1,0:T(8,128)(2,1)S(1)}, bf16[48,1152]{1,0:T(8,128)(2,1)S(1)}, u32[]{:S(2)}, u32[]{:S(2)}) collective-permute-start(bf16[48,1152]{1,0:T(8,128)(2,1)S(1)} %copy-done.26), channel_id=1, source_target_pairs={{0,4},{4,0},{1,5},{5,1},{2,6},{6,2},{3,7},{7,3},{8,12},{12,8},{9,1... | collective-permute-start | bytes 331784 | tf_op jit(solution)/shard_map/ppermute | solution.py:697
  305.9 5.2 %collective-permute-start.33 = (f32[8,1024]{1,0:T(8,128)S(1)}, f32[8,1024]{1,0:T(8,128)S(1)}, u32[]{:S(2)}, u32[]{:S(2)}) collective-permute-start(f32[8,1024]{1,0:T(8,128)S(1)} %add.199), channel_id=1, source_target_pairs={{0,1},{1,0},{2,3},{3,2},{4,5},{5,4},{6,7},{7,6},{8,9},{9,8},{10,11... | collective-permute-start | bytes 98312 | tf_op jit(solution)/shard_map/ppermute | solution.py:713
  306.0 6.1 %collective-permute-start.34 = (f32[8,1024]{1,0:T(8,128)S(1)}, f32[8,1024]{1,0:T(8,128)S(1)}, u32[]{:S(2)}, u32[]{:S(2)}) collective-permute-start(f32[8,1024]{1,0:T(8,128)S(1)} %add.199), channel_id=1, source_target_pairs={{0,2},{1,3},{2,0},{3,1},{4,6},{5,7},{6,4},{7,5},{8,10},{9,11},{10,... | collective-permute-start | bytes 98312 | tf_op jit(solution)/shard_map/ppermute | solution.py:713
  315.0 5.8 %collective-permute-start.38 = (f32[12,256]{1,0:T(8,128)S(1)}, f32[12,256]{1,0:T(8,128)S(1)}, u32[]{:S(2)}, u32[]{:S(2)}) collective-permute-start(f32[12,256]{1,0:T(8,128)S(1)} %get-tuple-element.165), channel_id=1, source_target_pairs={{0,1},{1,0},{2,3},{3,2},{4,5},{5,4},{6,7},{7,6},{8,9},{9,8},{10,11... | collective-permute-start | bytes 36872 | tf_op jit(solution)/shard_map/ppermute | solution.py:713
  315.3 5.6 %collective-permute-start.39 = (f32[12,256]{1,0:T(8,128)S(1)}, f32[12,256]{1,0:T(8,128)S(1)}, u32[]{:S(2)}, u32[]{:S(2)}) collective-permute-start(f32[12,256]{1,0:T(8,128)S(1)} %get-tuple-element.167), channel_id=1, source_target_pairs={{0,2},{1,3},{2,0},{3,1},{4,6},{5,7},{6,4},{7,5},{8,10},{9,11},{10,... | collective-permute-start | bytes 36872 | tf_op jit(solution)/shard_map/ppermute | solution.py:713
  320.1 6.3 %collective-permute-start.36 = (bf16[48,1536]{1,0:T(8,128)(2,1)S(1)}, bf16[48,1536]{1,0:T(8,128)(2,1)S(1)}, u32[]{:S(2)}, u32[]{:S(2)}) collective-permute-start(bf16[48,1536]{1,0:T(8,128)(2,1)S(1)} %dynamic-slice_bitcast_fusion), channel_id=1, source_target_pairs={{0,4},{4,0},{1,5},{5,1},{2,6},{6,2},{3,7},{7,3},{8,12},{12,8},{9,1... | collective-permute-start | bytes 442376 | tf_op jit(solution)/shard_map/ppermute | solution.py:697
  (39 other events, 511.6 us)
Sparse Core Ops, SparseCore 0:
  27.3 71.2 all-gather.1
  163.6 104.6 reduce-scatter.1
where the time goes:
time: 341 us; the launch traced here: 336 us
  Pallas kernels  126 us (37%)
  waiting for transfers between devices  120 us (35%)
  starting transfers between devices  45.3 us (13%)
  local copies, waits for them, and re-layouts  18.2 us (5%)
  between operations  14.6 us (4%)
  other arithmetic  10.9 us (3%)
    ppermute x29, waiting for transfers between devices, shift(): return lax.ppermute(value, axis, [(i, (i - by) % n) for i in range(n)])  92.6 us
    ppermute x29, starting transfers between devices, shift(): return lax.ppermute(value, axis, [(i, (i - by) % n) for i in range(n)])  30.9 us
    pallas_call x1, Pallas kernels, scan_backward(): pl.pallas_call(scan_backward_kernel, grid=(blocks,), in_specs=[pl.BlockSp...  30.4 us
    pallas_call x1, Pallas kernels, scan_forward(): pl.pallas_call(scan_forward_kernel, grid=(blocks,), in_specs=[pl.BlockSpe...  20.8 us
    all_gather x1, waiting for transfers between devices, per_device(): lax.all_gather(pair_rows(all_rows), ('y', 'x'), axis=0, tiled=True)  19.5 us
    pallas_call x2, Pallas kernels, token_grads(): pl.pallas_call(token_grads_kernel, grid_spec=pltpu.PrefetchScalarGridSpec...  16.9 us
    ppermute x12, starting transfers between devices, tensor_xor(): return lax.ppermute(value, TENSOR, [(i, i ^ by) for i in range(4)])  14.4 us
    pallas_call x1, Pallas kernels, mix_second(): pl.pallas_call(lambda *refs: mix_second_kernel(channels, *refs), grid_spe...  11.7 us
  transfers between devices with their start and end apart: 43, of which 22 were waited for; matrix products, arithmetic and copies ran while one was open for 6% of the time, Pallas kernels for 21%

commit v1 on v0

--- a/solution.py
+++ b/solution.py
@@ -65,11 +65,16 @@
     return total
 
 
-def spread_heads(cols, j, low_half):
-    return jnp.where(low_half, cols[:, 2 * j : 2 * j + 1], cols[:, 2 * j + 1 : 2 * j + 2])
-
-
-def scan_forward_kernel(tok, weights_a, weights_b, weights_c, taps, heads, chan, aux, segrow, pre_out, scan_out, state_out, ext, act, carry, fed):
+def two_parts(value):
+    high = value.astype(BF16)
+    return jnp.concatenate([high, (value - high.astype(F32)).astype(BF16)], 1)
+
+
+def spread_heads(cols, table):
+    return dot(two_parts(cols), table)
+
+
+def scan_forward_kernel(tok, weights_a, weights_b, weights_c, taps, heads, chan, spread, aux, segrow, pre_out, scan_out, state_out, ext, act, carry, fed):
     n = tok.shape[0]
     pairs = carry.shape[1] // 128
 
@@ -104,6 +109,7 @@
     enters = jnp.exp(cum) * marks[:, 3:4]
     to_end = jnp.exp(last - cum) * marks[:, 4:5]
     keep = jnp.exp(last) * marks[n - 1 : n, 3:4]
+    wide_cols = spread_heads(jnp.concatenate([step, enters, to_end, jnp.broadcast_to(keep, (8, 128))], 0), spread[...])
     held = carry[...]
     held_low = held.astype(BF16)
     state_out[0] = held_low
@@ -112,7 +118,7 @@
     for j in range(pairs):
         lanes = slice(j * 128, (j + 1) * 128)
         x = act[:, lanes]
-        xdt = x * spread_heads(step, j, low_half)
+        xdt = x * wide_cols[:n, lanes]
         parts = []
         for h in (2 * j, 2 * j + 1):
             decay = jnp.exp(jnp.minimum(cum[:, h : h + 1] - cum_t[h : h + 1, :], 0.0))
@@ -121,14 +127,14 @@
         zero = jnp.zeros_like(xdt_low)
         pair = jnp.concatenate([jnp.where(low_half, xdt_low, zero), jnp.where(low_half, zero, xdt_low)], 0)
         y = dot(jnp.concatenate(parts, 1), pair)
-        y += spread_heads(enters, j, low_half) * from_state[:, lanes] + chan[0:1, lanes] * x
+        y += wide_cols[n : 2 * n, lanes] * from_state[:, lanes] + chan[0:1, lanes] * x
         scan_out[:, lanes] = y
-        fed[:, lanes] = (xdt * spread_heads(to_end, j, low_half)).astype(BF16)
-        carry[:, lanes] = held[:, lanes] * spread_heads(keep, j, low_half)
+        fed[:, lanes] = (xdt * wide_cols[2 * n : 3 * n, lanes]).astype(BF16)
+        carry[:, lanes] = held[:, lanes] * wide_cols[3 * n : 3 * n + 1, lanes]
     carry[...] += dot(write_t, fed[...])
 
 
-def scan_backward_kernel(pre, pre_before, taps, heads, chan, sums, aux, segrow, grad, state, low_out, taps_out, heads_out, ext, gext, act, slope, carry, fed, back, rows):
+def scan_backward_kernel(pre, pre_before, taps, heads, chan, sums, spread, aux, segrow, grad, state, low_out, taps_out, heads_out, ext, gext, act, slope, carry, fed, back, rows):
     n = pre.shape[0]
     pairs = carry.shape[1] // 128
     wide = ext.shape[1]
@@ -171,6 +177,7 @@
     enters = jnp.exp(cum) * marks[:, 3:4]
     to_end = jnp.exp(last - cum) * marks[:, 4:5]
     keep = jnp.exp(last) * marks[n - 1 : n, 3:4]
+    wide_cols = spread_heads(jnp.concatenate([step, enters, to_end, jnp.broadcast_to(keep, (8, 128))], 0), spread[...])
     held = state[0]
     later = carry[...]
     later_low = later.astype(BF16)
@@ -187,15 +194,13 @@
     keep_part = jnp.zeros((8, 128), F32)
 
     def head_sums(value, j):
-        high = value.astype(BF16)
-        rest = (value - high.astype(F32)).astype(BF16)
-        return dot(jnp.concatenate([high, rest], 1), sums[j])
+        return dot(two_parts(value), sums[j])
 
     for j in range(pairs):
         lanes = slice(j * 128, (j + 1) * 128)
         x = act[:, lanes]
         dy = grad[:, lanes].astype(F32)
-        step_wide = spread_heads(step, j, low_half)
+        step_wide = wide_cols[:n, lanes]
         xdt = x * step_wide
         xdt_low = xdt.astype(BF16)
         dy_low = dy.astype(BF16)
@@ -216,8 +221,8 @@
             parts.append((decay * inner_t).astype(BF16))
         grad_pair = jnp.concatenate([jnp.where(low_half, dy_low, zero), jnp.where(low_half, zero, dy_low)], 0)
         grad_xdt = dot(jnp.concatenate(parts, 1), grad_pair)
-        end_wide = spread_heads(to_end, j, low_half)
-        enter_wide = spread_heads(enters, j, low_half)
+        end_wide = wide_cols[2 * n : 3 * n, lanes]
+        enter_wide = wide_cols[n : 2 * n, lanes]
         later_part = end_wide * from_later[:, lanes]
         grad_xdt += later_part
         to_end_part += head_sums(later_part * xdt, j)
@@ -230,7 +235,7 @@
         kept = jnp.sum(held[:, lanes].astype(F32) * later[:, lanes], axis=0, keepdims=True)
         keep_part += head_sums(jnp.broadcast_to(kept, (8, 128)), j)
         act[:, lanes] = grad_xdt * step_wide + chan[0:1, lanes] * dy
-        carry[:, lanes] = later[:, lanes] * spread_heads(keep, j, low_half)
+        carry[:, lanes] = later[:, lanes] * wide_cols[3 * n : 3 * n + 1, lanes]
 
     grad_cum = rows[...].T - col_sums + enter_part - to_end_part
     grad_last = jnp.sum(to_end_part, axis=0, keepdims=True) + keep * keep_part[0:1, :]
@@ -281,7 +286,7 @@
     return jnp.pad(marks, ((0, 0), (0, 128 - len(cols)))), jnp.broadcast_to(segments.astype(F32), (8, length))
 
 
-def scan_forward(tokens, weights, taps, heads, chan, marks, segrow):
+def scan_forward(tokens, weights, taps, heads, chan, spread, marks, segrow):
     length, model = tokens.shape
     cols = 1152
     inner = cols - 384
@@ -299,6 +304,7 @@
             whole((8, wide)),
             whole((8, 128)),
             whole((8, inner)),
+            whole((256, inner)),
             pl.BlockSpec((n, 128), lambda i: (i, 0)),
             pl.BlockSpec((8, n), lambda i: (0, i)),
         ],
@@ -321,10 +327,10 @@
         compiler_params=PARAMS,
         cost_estimate=cost(20),
         name="scan_forward",
-    )(tokens, weights, weights, weights, taps, heads, chan, marks, segrow)
-
-
-def scan_backward(pre, taps, heads, chan, sums, marks, segrow, grad, states):
+    )(tokens, weights, weights, weights, taps, heads, chan, spread, marks, segrow)
+
+
+def scan_backward(pre, taps, heads, chan, sums, spread, marks, segrow, grad, states):
     length, cols = pre.shape
     inner = cols - 384
     wide = cols - 128
@@ -345,6 +351,7 @@
             whole((8, 128)),
             whole((8, inner)),
             whole((inner // 128, 256, 128)),
+            whole((256, inner)),
             pl.BlockSpec((n, 128), lambda i: (rev(i), 0)),
             pl.BlockSpec((8, n), lambda i: (0, rev(i))),
             pl.BlockSpec((n, inner), lambda i: (rev(i), 0)),
@@ -373,7 +380,12 @@
         compiler_params=PARAMS,
         cost_estimate=cost(30),
         name="scan_backward",
-    )(pre, pre, taps, heads, chan, sums, marks, segrow, grad, states)
+    )(pre, pre, taps, heads, chan, sums, spread, marks, segrow, grad, states)
+
+
+def spread_table(inner):
+    head = jnp.arange(inner) // 64
+    return (jnp.arange(256)[:, None] % 128 == head[None, :]).astype(BF16)
 
 
 def head_sum_table(inner):
@@ -504,23 +516,23 @@
     store_block(total.astype(BF16), outs)
 
 
-def token_grads(grad_gate, low, weights, spot, first):
+def token_grads(grad_gate, low, weights, spot):
     model = weights.shape[0]
     width = grad_gate.shape[1]
     n = 256
 
     def rows(cols):
-        return pl.BlockSpec((n, cols), lambda i, me: (me[0] ^ (first - i), 0))
+        return pl.BlockSpec((n, cols), lambda i, me: (me[0] ^ (3 - i), 0))
 
     return pl.pallas_call(
         token_grads_kernel,
         grid_spec=pltpu.PrefetchScalarGridSpec(
             num_scalar_prefetch=1,
-            grid=(2,),
+            grid=(4,),
             in_specs=[rows(width), rows(low.shape[1]), column_block(model, width, 0), *first_specs(model)],
-            out_specs=[whole((n, model))] * 2,
+            out_specs=[whole((n, model))] * 4,
         ),
-        out_shape=[jax.ShapeDtypeStruct((n, model), BF16)] * 2,
+        out_shape=[jax.ShapeDtypeStruct((n, model), BF16)] * 4,
         compiler_params=PARAMS,
         cost_estimate=cost(6),
         name="token_grads",
@@ -559,21 +571,29 @@
 
 
 def first_grads_kernel(me, tok, low, weights_a, weights_b, weights_c, gate_gains, norm_gain, taps, heads, gain, *rest):
-    *outs, packed, gains = rest
+    outs_a, outs_b = rest[:4], rest[4:8]
+    packed, gains, held = rest[8:]
     step = pl.program_id(0)
+    y = (me[0] + step) % 4
+    n = tok.shape[1]
+    cut = outs_a[0].shape[2]
+    deep = n // 4
     grad = lax.dot_general(tok[...], low[...], TN, preferred_element_type=F32)
-    total = jnp.zeros((grad.shape[0], 128), F32)
-    for n, w in enumerate((weights_a, weights_b, weights_c)):
+    total = jnp.zeros((n, 128), F32)
+    for block, w in enumerate((weights_a, weights_b, weights_c)):
         for m in range(3):
-            product = grad[:, 384 * n + 128 * m : 384 * n + 128 * (m + 1)] * w[:, 128 * m : 128 * (m + 1)].astype(F32)
-            total += product
-    spot = pl.ds(pl.multiple_of(((me[0] + step) % 4) * grad.shape[0], 128), grad.shape[0])
-    gains[0:1, spot] = row_sums(total)
+            lanes = slice(384 * block + 128 * m, 384 * block + 128 * (m + 1))
+            total += grad[:, lanes] * w[:, 128 * m : 128 * (m + 1)].astype(F32)
+    gains[0:1, pl.ds(pl.multiple_of(y * n, 128), n)] = row_sums(total)
     for k in range(4):
 
         @pl.when(step == k)
         def _():
-            outs[k][...] = grad.astype(BF16).reshape(outs[k].shape)
+            outs_a[k][...] = grad[:, :cut].astype(BF16).reshape(outs_a[k].shape)
+
+    held[...] = grad[:, cut:].astype(BF16)
+    for k in range(4):
+        outs_b[k][y] = held[pl.ds(pl.multiple_of(((me[1] + k) % 4) * deep, 16), deep), :]
 
     @pl.when(step == 3)
     def _():
@@ -592,8 +612,9 @@
 def first_grads(tokens, low, weights, gate_gains, norm_gain, taps, heads, gain, me):
     length, model = tokens.shape
     width = low.shape[1]
+    cut = 640
     n = model // 4
-    shape = (4, n // 4, width)
+    shape_a, shape_b = (4, n // 4, cut), (4, n // 4, width - cut)
 
     def spot(i, me):
         return (me[0] + i) % 4
@@ -615,47 +636,59 @@
                 whole(heads.shape),
                 whole(gain.shape),
             ],
-            out_specs=[whole(shape)] * 4 + [whole((8, 1024))],
-            scratch_shapes=[pltpu.VMEM((8, model), F32)],
+            out_specs=[whole(shape_a)] * 4 + [whole(shape_b)] * 4 + [whole((8, 1024))],
+            scratch_shapes=[pltpu.VMEM((8, model), F32), pltpu.VMEM((n, width - cut), BF16)],
         ),
-        out_shape=[jax.ShapeDtypeStruct(shape, BF16)] * 4 + [jax.ShapeDtypeStruct((8, 1024), F32)],
+        out_shape=[jax.ShapeDtypeStruct(shape_a, BF16)] * 4
+        + [jax.ShapeDtypeStruct(shape_b, BF16)] * 4
+        + [jax.ShapeDtypeStruct((8, 1024), F32)],
         compiler_params=PARAMS,
         cost_estimate=cost(6),
         name="first_grads",
     )(me, tokens, low, weights, weights, weights, gate_gains, norm_gain, taps, heads, gain)
 
 
-def add_split_kernel(me, own, ahead, across, behind, *outs):
-    for d in range(4):
-        e = (me[0] + d) % 4
-        total = (own[e].astype(F32) + across[e].astype(F32)) + (ahead[e].astype(F32) + behind[e].astype(F32))
-        outs[d][...] = total.astype(BF16)
-
-
-def add_split(parts, me):
-    shape = parts[0].shape[1:]
-    return pl.pallas_call(
+def four_sum(own, ahead, across, behind):
+    return (own.astype(F32) + across.astype(F32)) + (ahead.astype(F32) + behind.astype(F32))
+
+
+def add_split_kernel(me, *refs):
+    ins, outs = refs[:8], refs[8:]
+    for half in range(2):
+        for d in range(4):
+            e = (me[half] + d) % 4
+            outs[4 * half + d][...] = four_sum(*[part[e] for part in ins[4 * half : 4 * half + 4]]).astype(BF16)
+
+
+def add_split(parts_a, parts_b, me):
+    shapes = [jax.ShapeDtypeStruct(parts[0].shape[1:], BF16) for parts in (parts_a, parts_b) for _ in range(4)]
+    outs = pl.pallas_call(
         add_split_kernel,
-        in_specs=[pl.BlockSpec(memory_space=pltpu.SMEM)] + [VMEM_SPEC] * 4,
-        out_specs=[VMEM_SPEC] * 4,
-        out_shape=[jax.ShapeDtypeStruct(shape, BF16)] * 4,
+        in_specs=[pl.BlockSpec(memory_space=pltpu.SMEM)] + [VMEM_SPEC] * 8,
+        out_specs=[VMEM_SPEC] * 8,
+        out_shape=shapes,
         compiler_params=PARAMS,
         name="add_split",
-    )(me, *parts)
-
-
-def add_halve_kernel(me, own, ahead, across, behind, keep, give, total):
-    total[...] = (own[...].astype(F32) + across[...].astype(F32)) + (ahead[...].astype(F32) + behind[...].astype(F32))
+    )(me, *parts_a, *parts_b)
+    return outs[:4], outs[4:]
+
+
+def add_halve_kernel(me, *refs):
+    ins, (keep, give, total) = refs[:8], refs[8:]
+    cut = ins[0].shape[1]
+    total[:, :cut] = four_sum(*[part[...] for part in ins[:4]])
+    total[:, cut:] = four_sum(*[part[...] for part in ins[4:]])
     n = keep.shape[0]
     keep[...] = total[pl.ds(pl.multiple_of(me[0] * n, 16), n), :]
     give[...] = total[pl.ds(pl.multiple_of((1 - me[0]) * n, 16), n), :].astype(BF16)
 
 
-def add_halve(parts, me):
-    rows, width = parts[0].shape
+def add_halve(parts_a, parts_b, me):
+    rows = parts_a[0].shape[0]
+    width = parts_a[0].shape[1] + parts_b[0].shape[1]
     return pl.pallas_call(
         add_halve_kernel,
-        in_specs=[pl.BlockSpec(memory_space=pltpu.SMEM)] + [VMEM_SPEC] * 4,
+        in_specs=[pl.BlockSpec(memory_space=pltpu.SMEM)] + [VMEM_SPEC] * 8,
         out_specs=[VMEM_SPEC] * 2,
         out_shape=[
             jax.ShapeDtypeStruct((rows // 2, width), F32),
@@ -664,7 +697,7 @@
         scratch_shapes=[pltpu.VMEM((rows, width), F32)],
         compiler_params=PARAMS,
         name="add_halve",
-    )(me, *parts)
+    )(me, *parts_a, *parts_b)
 
 
 def place_kernel(me, *refs):
@@ -794,8 +827,10 @@
     gain = jnp.broadcast_to(gated_gain, (8, width))
     norm_rows = jnp.broadcast_to(norm_gain, (8, model_width))
     marks, segrow = scan_marks(segments)
+    spread = spread_table(width)
+    sum_table = head_sum_table(width)
     tokens, grad_rows = lax.optimization_barrier((tokens, grad_rows))
-    pre, scanned, states = scan_forward(tokens, weights, taps, head_rows, chan, marks, segrow)
+    pre, scanned, states = scan_forward(tokens, weights, taps, head_rows, chan, spread, marks, segrow)
 
     gate_pre, grad_mixed, sums = mix_first(tokens, grad_rows, weights, scanned, gain)
     sums = (sums + tensor_xor(sums, 1)) + (tensor_xor(sums, 2) + tensor_xor(sums, 3))
@@ -808,32 +843,40 @@
     second_sum = lax.psum_scatter(second_total, ("y", "x"), scatter_dimension=0, tiled=True)
     out_far_got = swap(out_far, "zh")
 
-    sum_table = head_sum_table(width)
     grad_scanned = after(grad_scanned, out_far, second_total)
     low, tap_sums, head_sums = scan_backward(
-        pre, taps, head_rows, chan, sum_table, marks, segrow, grad_scanned, states
+        pre, taps, head_rows, chan, sum_table, spread, marks, segrow, grad_scanned, states
     )
     low = after(low, out_far_got)
     *first_blocks, small = first_grads(
-        tokens, low, weights, gate_gains, norm_rows, tap_sums, head_sums, gain_sums, me["y"]
+        tokens,
+        low,
+        weights,
+        gate_gains,
+        norm_rows,
+        tap_sums,
+        head_sums,
+        gain_sums,
+        jnp.concatenate([me["y"], me["x"]]),
     )
-    first_parts = sends(first_blocks, "y")
+    parts_a = sends(first_blocks[:4], "y")
+    parts_b = sends(first_blocks[4:], "x")
     low_late = after(low, *first_blocks)
-    far_give, far_keep = token_grads(gate_grad_low, low_late, weights, spot, 3)
-    far_got = jnp.concatenate([swap(far_give[:128], "c"), swap(far_give[128:], "c")], 0)
-    near_give, near_keep = token_grads(gate_grad_low, after(low_late, far_give), weights, spot, 1)
-    near_got = swap(near_give, "c")
-    row_far = (far_keep.astype(F32) + far_got.astype(F32)).astype(BF16)
+    row_blocks = token_grads(gate_grad_low, low_late, weights, spot)
+    parts_a = [after(part, *row_blocks) for part in parts_a]
+    parts_b = [after(part, *row_blocks) for part in parts_b]
+    half_a, half_b = add_split(parts_a, parts_b, jnp.concatenate([me["x"], me["y"]]))
+    far_got = swap(after(row_blocks[0], *half_a), "c")
+    near_got = swap(row_blocks[2], "c")
+    row_far = (row_blocks[1].astype(F32) + far_got.astype(F32)).astype(BF16)
     row_far_got = swap(row_far, "zh")
-
-    first_parts = [after(part, row_far_got, near_give) for part in first_parts]
-    first_halves = add_split(first_parts, me["x"])
-    first_parts = sends(first_halves, "x")
-    small = sum_ring(after(small, *first_halves), "y")
-    first_keep, first_give = add_halve(first_parts, me["zl"])
+    parts_a = [after(part, row_far) for part in sends(half_a, "x")]
+    parts_b = [after(part, row_far) for part in sends(half_b, "y")]
+    small = sum_ring(after(small, *half_a), "y")
+    first_keep, first_give = add_halve(parts_a, parts_b, me["zl"])
+    first_mine = first_keep + swap(first_give, "zl").astype(F32)
     small = sum_ring(after(small, first_give), "x")
     small = sum_pair(small, "zl")
-    first_mine = first_keep + swap(first_give, "zl").astype(F32)
     second_pairs = second_sum.reshape(2, 48, 2 * width)
     second_keep = lax.dynamic_index_in_dim(second_pairs, me["zl"][0], 0, keepdims=False)
     second_mine = second_keep.astype(F32) + swap(
@@ -843,7 +886,7 @@
     hidden_out = (
         residual_in + (out_blocks[3].astype(F32) + out_near.astype(F32) + out_far_got.astype(F32))
     ).astype(BF16)
-    grad_normed = near_keep.astype(F32) + near_got.astype(F32) + row_far_got.astype(F32)
+    grad_normed = row_blocks[3].astype(F32) + near_got.astype(F32) + row_far_got.astype(F32)
     weighted = jnp.sum(grad_normed * norm_gain * residual_in, axis=-1, keepdims=True)
     grad_hidden = (
         out_grad.astype(F32)
@@ -861,6 +904,7 @@
         tensor_xor(quarter(2), 2) + tensor_xor(quarter(3), 3)
     )
 
+    small = after(small, row_far_got, second_mine)
     summed = (small + tensor_xor(small, 1)) + (tensor_xor(small, 2) + tensor_xor(small, 3))
     grad_norm_gain = jnp.concatenate([summed[6], summed[7, :512]])
     return (

time: 341 us -> 331 us (0.971)
  waiting for transfers between devices: 120 us -> 95.8 us
  starting transfers between devices: 45.3 us -> 63.3 us
  Pallas kernels: 126 us -> 114 us
  other arithmetic: 10.9 us -> 16.4 us
  local copies, waits for them, and re-layouts: 18.2 us -> 22.8 us
    ppermute x29 -> x34, waiting for transfers between devices: 92.6 us -> 69.7 us  [shift(): return lax.ppermute(value, axis, [(i, (i - by) % n) for i in range(n)])]
    ppermute x29 -> x34, starting transfers between devices: 30.9 us -> 49 us  [shift(): return lax.ppermute(value, axis, [(i, (i - by) % n) for i in range(n)])]
    unnamed x63 -> x89, local copies, waits for them, and re-layouts: 6.04 us -> 11.9 us
    pallas_call x1, Pallas kernels: 30.4 us -> 24.7 us  [scan_backward(): pl.pallas_call(scan_backward_kernel, grid=(blocks,), in_specs=[pl.BlockSp...]
    pallas_call x2 -> x1, Pallas kernels: 16.9 us -> 13.3 us  [token_grads(): pl.pallas_call(token_grads_kernel, grid_spec=pltpu.PrefetchScalarGridSpec...]
    all_gather x1, waiting for transfers between devices: 19.5 us -> 16.1 us  [per_device(): lax.all_gather(pair_rows(all_rows), ('y', 'x'), axis=0, tiled=True)]
  transfers between devices with their start and end apart: 43 -> 48, of which waited for: 22 -> 17; matrix products, arithmetic and copies ran while one was open for 6% -> 8% of each run, Pallas kernels for 21% -> 19%
where the time goes in v1:
time: 331 us; the launch traced here: 327 us
  Pallas kernels  114 us (34%)
  waiting for transfers between devices  95.8 us (29%)
  starting transfers between devices  63.3 us (19%)
  local copies, waits for them, and re-layouts  22.8 us (7%)
  other arithmetic  16.4 us (5%)
  between operations  14.7 us (4%)
    ppermute x34, waiting for transfers between devices, shift(): return lax.ppermute(value, axis, [(i, (i - by) % n) for i in range(n)])  69.7 us
    ppermute x34, starting transfers between devices, shift(): return lax.ppermute(value, axis, [(i, (i - by) % n) for i in range(n)])  49 us
    pallas_call x1, Pallas kernels, scan_backward(): pl.pallas_call(scan_backward_kernel, grid=(blocks,), in_specs=[pl.BlockSp...  24.7 us
    pallas_call x1, Pallas kernels, scan_forward(): pl.pallas_call(scan_forward_kernel, grid=(blocks,), in_specs=[pl.BlockSpe...  17.4 us
    all_gather x1, waiting for transfers between devices, per_device(): lax.all_gather(pair_rows(all_rows), ('y', 'x'), axis=0, tiled=True)  16.1 us
    ppermute x12, starting transfers between devices, tensor_xor(): return lax.ppermute(value, TENSOR, [(i, i ^ by) for i in range(4)])  14.2 us
    pallas_call x1, Pallas kernels, token_grads(): pl.pallas_call(token_grads_kernel, grid_spec=pltpu.PrefetchScalarGridSpec...  13.3 us
    unnamed x89, local copies, waits for them, and re-layouts  11.9 us
  transfers between devices with their start and end apart: 48, of which 17 were waited for; matrix products, arithmetic and copies ran while one was open for 8% of the time, Pallas kernels for 19%

profile of v1, /device:TPU:24, one launch (start us, length us, event | category | flops | bytes accessed | tf_op | source)
XLA Modules:
  0.0 327.4 jit_solution(16482707728633049717)
XLA Ops:
  7.3 4.0 %collective-permute-start.7 = (bf16[12,256]{1,0:T(8,128)(2,1)}, bf16[12,256]{1,0:T(8,128)(2,1)S(1)}, u32[]{:S(2)}, u32[]{:S(2)}) collective-permute-start(bf16[12,256]{1,0:T(8,128)(2,1)} %param.17), channel_id=1, source_target_pairs={{0,2},{1,3},{2,0},{3,1},{4,6},{5,7},{6,4},{7,5},{8,10},{9,11},{10,... | collective-permute-start | bytes 18440 | tf_op jit(solution)/shard_map/ppermute | solution.py:746
  17.3 7.3 %collective-permute-done.9.refs_1_ = bf16[48,2688]{1,0:T(8,128)(2,1)S(1)} collective-permute-done((bf16[48,2688]{1,0:T(8,128)(2,1)S(1)}, bf16[48,2688]{1,0:T(8,128)(2,1)S(1)}, u32[]{:S(2)}, u32[]{:S(2)}) %collective-permute-start.9) | collective-permute-done | bytes 258080 | tf_op jit(solution)/shard_map/ppermute | solution.py:730
  28.4 3.2 collective-permute-start.1
  32.0 16.8 %collective-permute-done.1.refs_2_ = bf16[256,1536]{1,0:T(8,128)(2,1)S(1)} collective-permute-done((bf16[256,1536]{1,0:T(8,128)(2,1)S(1)}, bf16[256,1536]{1,0:T(8,128)(2,1)S(1)}, u32[]{:S(2)}, u32[]{:S(2)}) %collective-permute-start.1) | collective-permute-done | bytes 786464 | tf_op jit(solution)/shard_map/ppermute | solution.py:730
  49.7 3.2 collective-permute-start.4
  55.1 14.4 %collective-permute-done.4.refs_2_ = bf16[256,1536]{1,0:T(8,128)(2,1)} collective-permute-done((bf16[256,1536]{1,0:T(8,128)(2,1)S(1)}, bf16[256,1536]{1,0:T(8,128)(2,1)}, u32[]{:S(2)}, u32[]{:S(2)}) %collective-permute-start.4) | collective-permute-done | bytes 786464 | tf_op jit(solution)/shard_map/ppermute | solution.py:730
  72.5 4.1 %place_tokens.2.tok = bf16[1024,1536]{1,0:T(8,128)(2,1)} custom-call(s32[1]{0:T(128)} %bitcast.me.refs_0_, bf16[256,1536]{1,0:T(8,128)(2,1)} %copy-done.1, bf16[256,1536]{1,0:T(8,128)(2,1)} %collective-permute-done.refs_1_, bf16[256,1536]{1,0:T(8,128)(2,1)} %copy-done.5, bf16[256,1536]{1,0:T(8,128)(2,1)} %copy-done.8), custom_call_target="tpu_custom_call" | custom-call | flops 2000000 | bytes 6000 | tf_op jit(solution)/shard_map/place_tokens/pallas_call | solution.py:713
  78.4 4.1 %place_tokens.3.rows = bf16[1024,1536]{1,0:T(8,128)(2,1)} custom-call(s32[1]{0:T(128)} %bitcast.me.refs_0_, bf16[256,1536]{1,0:T(8,128)(2,1)} %refs_0_.1, bf16[256,1536]{1,0:T(8,128)(2,1)} %copy-done.6, bf16[256,1536]{1,0:T(8,128)(2,1)} %collective-permute-done.4.refs_2_, bf16[256,1536]{1,0:T(8,128)(2,1)} %copy-done.7), custom_call_target="tpu_custom_call" | custom-call | flops 2000000 | bytes 6000 | tf_op jit(solution)/shard_map/place_tokens/pallas_call | solution.py:713
  82.5 16.1 %all-gather.2.cloned.1.call-done.weights_a.weights_b.weights_c.gate_w.out_w.refs_5_ = bf16[1536,2688]{1,0:T(8,128)(2,1)} async-done(((bf16[96,2688]{1,0:T(8,128)(2,1)}), bf16[1536,2688]{1,0:T(8,128)(2,1)}) %all-gather.2.cloned.1.call-update) | async-done | bytes 8257552 | tf_op jit(solution)/shard_map/all_gather | solution.py:807
  99.8 17.4 %scan_forward.1 = (f32[1024,1152]{1,0:T(8,128)}, f32[1024,768]{1,0:T(8,128)}, bf16[8,128,768]{2,1,0:T(8,128)(2,1)}) custom-call(bf16[1024,1536]{1,0:T(8,128)(2,1)} %place_tokens.2.tok, bf16[1536,2688]{1,0:T(8,128)(2,1)} %all-gather.2.cloned.1.call-done.weights_a.weights_b.weights_c.gate_w.out_w.refs_5_, ...), custom_call_target="tpu_custom_call" | custom-call | flops 20000000 | bytes 60000 | tf_op jit(solution)/shard_map/scan_forward/pallas_call | solution.py:298
  117.8 10.6 %mix_first.1 = (f32[1024,768]{1,0:T(8,128)}, f32[1024,768]{1,0:T(8,128)}, f32[8,1024]{1,0:T(8,128)}) custom-call(bf16[1024,1536]{1,0:T(8,128)(2,1)} %place_tokens.2.tok, bf16[1024,1536]{1,0:T(8,128)(2,1)} %place_tokens.3.rows, bf16[1536,2688]{1,0:T(8,128)(2,1)} %all-gather.2.cloned.1.call-done.weights_a.weights_b.weights_c.gate_w.out_w.refs_5_, ...), custom_call_target="tpu_custom_call" | custom-call | flops 10000000 | bytes 30000 | tf_op jit(solution)/shard_map/mix_first/pallas_call | solution.py:419
  128.5 3.2 collective-permute-start.11
  131.9 2.3 collective-permute-done.11
  134.2 2.6 collective-permute-done.12
  138.2 11.7 %mix_second.1 = (bf16[1024,768]{1,0:T(8,128)(2,1)}, f32[1024,768]{1,0:T(8,128)}, bf16[1024,768]{1,0:T(8,128)(2,1)}, f32[8,768]{1,0:T(8,128)}, bf16[256,1536]{1,0...) custom-call(s32[1]{0:T(128)} %bitcast.me.refs_0_, ...), custom_call_target="tpu_custom_call" | custom-call | flops 11000000 | bytes 33000 | tf_op jit(solution)/shard_map/mix_second/pallas_call | solution.py:484
  149.9 10.2 %second_grads.1 = (bf16[1536,1536]{1,0:T(8,128)(2,1)}, f32[8,1536]{1,0:T(8,128)}) custom-call(bf16[1024,1536]{1,0:T(8,128)(2,1)} %place_tokens.2.tok, bf16[1024,1536]{1,0:T(8,128)(2,1)} %place_tokens.3.rows, bf16[1024,768]{1,0:T(8,128)(2,1)} %get-tuple-element.92.grad_gate, bf16[1024,768]{1,0:T(8,128)(2,1)} %get-tuple-element.95.mixed, ...), custom_call_target="tpu_custom_call" | custom-call | flops 8000000 | bytes 24000 | tf_op jit(solution)/shard_map/second_grads/pallas_call | solution.py:561
  166.3 24.7 %scan_backward.1 = (bf16[1024,1152]{1,0:T(8,128)(2,1)}, f32[8,1024]{1,0:T(8,128)}, f32[8,128]{1,0:T(8,128)}) custom-call(f32[1024,1152]{1,0:T(8,128)} %get-tuple-element.93.pre.pre_before, f32[1024,1152]{1,0:T(8,128)} %get-tuple-element.93.pre.pre_before, f32[8,1024]{1,0:T(8,128)} %select_maximum_fusion.taps, f32[8,128]{1,0:T(8,128)} %select_maximum_fusion.1.heads, ...), custom_call_target="tpu_custom_call" | custom-call | flops 30000000 | bytes 90000 | tf_op jit(solution)/shard_map/scan_backward/pallas_call | solution.py:344
  191.7 11.0 %first_grads.1 = (bf16[4,96,640]{2,1,0:T(8,128)(2,1)}, bf16[4,96,640]{2,1,0:T(8,128)(2,1)}, bf16[4,96,640]{2,1,0:T(8,128)(2,1)}, bf16[4,96,640]{2,1,0:T(8,128)(2...) custom-call(s32[2]{0:T(128)} %pad_add_fusion.1.me, ...), custom_call_target="tpu_custom_call" | custom-call | flops 6000000 | bytes 18000 | tf_op jit(solution)/shard_map/first_grads/pallas_call | solution.py:622
  204.6 2.9 collective-permute-start.18
  209.0 7.5 %collective-permute-done.22.refs_7_ = bf16[4,96,512]{2,1,0:T(8,128)(2,1)S(1)} collective-permute-done((bf16[4,96,512]{2,1,0:T(8,128)(2,1)}, bf16[4,96,512]{2,1,0:T(8,128)(2,1)S(1)}, u32[]{:S(2)}, u32[]{:S(2)}) %collective-permute-start.22) | collective-permute-done | bytes 393248 | tf_op jit(solution)/shard_map/ppermute | solution.py:730
  217.5 13.3 %token_grads.1 = (bf16[256,1536]{1,0:T(8,128)(2,1)}, bf16[256,1536]{1,0:T(8,128)(2,1)}, bf16[256,1536]{1,0:T(8,128)(2,1)}, bf16[256,1536]{1,0:T(8,128)(2,1)}) custom-call(s32[1]{0:T(128)} %bitcast.me.refs_0_, bf16[1024,768]{1,0:T(8,128)(2,1)} %get-tuple-element.92.grad_gate, bf16[1024,1152]{1,0:T(8,128)(2,1)} %get-tuple-element.113.low, ...), custom_call_target="tpu_custom_call" | custom-call | flops 6000000 | bytes 18000 | tf_op jit(solution)/shard_map/token_grads/pallas_call | solution.py:527
  232.8 3.1 add_split.1
  237.2 7.7 %collective-permute-start.26 = (f32[8,1024]{1,0:T(8,128)S(1)}, f32[8,1024]{1,0:T(8,128)S(1)}, u32[]{:S(2)}, u32[]{:S(2)}) collective-permute-start(f32[8,1024]{1,0:T(8,128)S(1)} %copy-done.29), channel_id=1, source_target_pairs={{0,96},{32,0},{64,32},{96,64},{1,97},{33,1},{65,33},{97,65},{2,98}... | collective-permute-start | bytes 98312 | tf_op jit(solution)/shard_map/ppermute | solution.py:730
  244.8 3.5 %collective-permute-start.30 = (bf16[96,640]{1,0:T(8,128)(2,1)}, bf16[96,640]{1,0:T(8,128)(2,1)S(1)}, u32[]{:S(2)}, u32[]{:S(2)}) collective-permute-start(bf16[96,640]{1,0:T(8,128)(2,1)} %get-tuple-element.129), channel_id=1, source_target_pairs={{0,24},{8,0},{16,8},{24,16},{1,25},{9,1},{17,9},{25,17},{2,26},{10... | collective-permute-start | bytes 368648 | tf_op jit(solution)/shard_map/ppermute | solution.py:730
  253.3 4.1 %collective-permute-done.33.refs_7_ = bf16[96,512]{1,0:T(8,128)(2,1)S(1)} collective-permute-done((bf16[96,512]{1,0:T(8,128)(2,1)}, bf16[96,512]{1,0:T(8,128)(2,1)S(1)}, u32[]{:S(2)}, u32[]{:S(2)}) %collective-permute-start.33) | collective-permute-done | bytes 98336 | tf_op jit(solution)/shard_map/ppermute | solution.py:730
  258.6 2.2 collective-permute-start.31
  271.7 2.3 collective-permute-start.42
  274.0 3.6 %collective-permute-start.24 = (bf16[256,1536]{1,0:T(8,128)(2,1)}, bf16[256,1536]{1,0:T(8,128)(2,1)}, u32[]{:S(2)}, u32[]{:S(2)}) collective-permute-start(bf16[256,1536]{1,0:T(8,128)(2,1)} %add_convert_fusion), channel_id=1, source_target_pairs={{0,2},{2,0},{1,3},{3,1},{4,6},{6,4},{5,7},{7,5},{8,10},{10,8},{9,1... | collective-permute-start | bytes 2359304 | tf_op jit(solution)/shard_map/ppermute | solution.py:730
  280.8 14.7 %collective-permute-done.37 = f32[8,1024]{1,0:T(8,128)S(1)} collective-permute-done((f32[8,1024]{1,0:T(8,128)S(1)}, f32[8,1024]{1,0:T(8,128)S(1)}, u32[]{:S(2)}, u32[]{:S(2)}) %collective-permute-start.37) | collective-permute-done | bytes 32800 | tf_op jit(solution)/shard_map/ppermute | solution.py:730
  295.5 3.3 collective-permute-start.44
  300.7 2.7 collective-permute-done.45
  307.5 4.1 %fusion.7 = (bf16[256,1536]{1,0:T(8,128)(2,1)}, bf16[256,1536]{1,0:T(8,128)(2,1)}) fusion(bf16[256,1536]{1,0:T(8,128)(2,1)S(1)} %copy-done, bf16[256,1536]{1,0:T(8,128)(2,1)S(1)} %copy-done.3, bf16[256,1536]{1,0:T(8,128)(2,1)} %collective-permute-done.24, bf16[256,1536]{1,0:T(8,128)(2,1)S(1)} %collective-permute-done.16, bf16[256,1536]{1,0:T(8,128)(2,1)S(1)} %copy-done.4, ...), kind=kLoop, calls=%fused_computation.12 | loop fusion | flops 8650752 | bytes 7873536 | tf_op jit(solution)/shard_map/convert_element_type | solution.py:895
  (232 shorter events, 70.6 us)
Async XLA Ops:
  7.2 91.4 %all-gather.2.cloned.1.call-start = ((), (), s32[]{:S(2)}) async-start(), calls=%async_computation.1 | async-start | bytes 8773632 | tf_op jit(solution)/shard_map/all_gather | solution.py:807
  7.2 8.0 %collective-permute-start.6 = (bf16[12,256]{1,0:T(8,128)(2,1)}, bf16[12,256]{1,0:T(8,128)(2,1)S(1)}, u32[]{:S(2)}, u32[]{:S(2)}) collective-permute-start(bf16[12,256]{1,0:T(8,128)(2,1)} %param.17), channel_id=1, source_target_pairs={{0,1},{1,0},{2,3},{3,2},{4,5},{5,4},{6,7},{7,6},{8,9},{9,8},{10,11... | collective-permute-start | bytes 18440 | tf_op jit(solution)/shard_map/ppermute | solution.py:746
  7.3 8.1 %collective-permute-start.7 = (bf16[12,256]{1,0:T(8,128)(2,1)}, bf16[12,256]{1,0:T(8,128)(2,1)S(1)}, u32[]{:S(2)}, u32[]{:S(2)}) collective-permute-start(bf16[12,256]{1,0:T(8,128)(2,1)} %param.17), channel_id=1, source_target_pairs={{0,2},{1,3},{2,0},{3,1},{4,6},{5,7},{6,4},{7,5},{8,10},{9,11},{10,... | collective-permute-start | bytes 18440 | tf_op jit(solution)/shard_map/ppermute | solution.py:746
  16.2 8.4 %collective-permute-start.9 = (bf16[48,2688]{1,0:T(8,128)(2,1)S(1)}, bf16[48,2688]{1,0:T(8,128)(2,1)S(1)}, u32[]{:S(2)}, u32[]{:S(2)}) collective-permute-start(bf16[48,2688]{1,0:T(8,128)(2,1)S(1)} %pad_dynamic-update-slice_fusion.refs_0_), channel_id=1, source_target_pairs={{0,4},{4,0},{1,5},{5,1},{2,6},{6,2},{3,7},{7,3},{8,12},{12,8},{9,1... | collective-permute-start | bytes 774152 | tf_op jit(solution)/shard_map/ppermute | solution.py:730
  27.2 278.6 %reduce-scatter.2.cloned.1.call-start = ((), (), s32[]{:S(2)}) async-start(), calls=%async_computation.2 | async-start | bytes 5013504 | tf_op jit(solution)/shard_map/reduce_scatter | solution.py:843
  28.4 20.4 %collective-permute-start.1 = (bf16[256,1536]{1,0:T(8,128)(2,1)S(1)}, bf16[256,1536]{1,0:T(8,128)(2,1)S(1)}, u32[]{:S(2)}, u32[]{:S(2)}) collective-permute-start(bf16[256,1536]{1,0:T(8,128)(2,1)S(1)} %fusion.2.refs_0_), channel_id=1, source_target_pairs={{0,2},{2,0},{1,3},{3,1},{4,6},{6,4},{5,7},{7,5},{8,10},{10,8},{9,1... | collective-permute-start | bytes 2359304 | tf_op jit(solution)/shard_map/ppermute | solution.py:730
  31.5 40.1 %collective-permute-start = (bf16[256,1536]{1,0:T(8,128)(2,1)S(1)}, bf16[256,1536]{1,0:T(8,128)(2,1)}, u32[]{:S(2)}, u32[]{:S(2)}) collective-permute-start(bf16[256,1536]{1,0:T(8,128)(2,1)S(1)} %fusion.2.refs_0_), channel_id=1, source_target_pairs={{0,1},{1,0},{2,3},{3,2},{4,5},{5,4},{6,7},{7,6},{8,9},{9,8},{10,11... | collective-permute-start | bytes 2359304 | tf_op jit(solution)/shard_map/ppermute | solution.py:730
  49.7 19.8 %collective-permute-start.4 = (bf16[256,1536]{1,0:T(8,128)(2,1)S(1)}, bf16[256,1536]{1,0:T(8,128)(2,1)}, u32[]{:S(2)}, u32[]{:S(2)}) collective-permute-start(bf16[256,1536]{1,0:T(8,128)(2,1)S(1)} %copy-done.2), channel_id=1, source_target_pairs={{0,2},{2,0},{1,3},{3,1},{4,6},{6,4},{5,7},{7,5},{8,10},{10,8},{9,1... | collective-permute-start | bytes 2359304 | tf_op jit(solution)/shard_map/ppermute | solution.py:730
  54.6 22.0 %collective-permute-start.3 = (bf16[256,1536]{1,0:T(8,128)(2,1)S(1)}, bf16[256,1536]{1,0:T(8,128)(2,1)S(1)}, u32[]{:S(2)}, u32[]{:S(2)}) collective-permute-start(bf16[256,1536]{1,0:T(8,128)(2,1)S(1)} %copy-done.2), channel_id=1, source_target_pairs={{0,1},{1,0},{2,3},{3,2},{4,5},{5,4},{6,7},{7,6},{8,9},{9,8},{10,11... | collective-permute-start | bytes 2359304 | tf_op jit(solution)/shard_map/ppermute | solution.py:730
  54.6 17.1 %collective-permute-start.2 = (bf16[256,1536]{1,0:T(8,128)(2,1)}, bf16[256,1536]{1,0:T(8,128)(2,1)S(1)}, u32[]{:S(2)}, u32[]{:S(2)}) collective-permute-start(bf16[256,1536]{1,0:T(8,128)(2,1)} %copy-done.5), channel_id=1, source_target_pairs={{0,1},{1,0},{2,3},{3,2},{4,5},{5,4},{6,7},{7,6},{8,9},{9,8},{10,11... | collective-permute-start | bytes 2359304 | tf_op jit(solution)/shard_map/ppermute | solution.py:730
  69.5 7.1 %collective-permute-start.5 = (bf16[256,1536]{1,0:T(8,128)(2,1)}, bf16[256,1536]{1,0:T(8,128)(2,1)S(1)}, u32[]{:S(2)}, u32[]{:S(2)}) collective-permute-start(bf16[256,1536]{1,0:T(8,128)(2,1)} %collective-permute-done.4.refs_2_), channel_id=1, source_target_pairs={{0,1},{1,0},{2,3},{3,2},{4,5},{5,4},{6,7},{7,6},{8,9},{9,8},{10,11... | collective-permute-start | bytes 2359304 | tf_op jit(solution)/shard_map/ppermute | solution.py:730
  163.8 27.2 %collective-permute-start.15 = (bf16[256,1536]{1,0:T(8,128)(2,1)S(1)}, bf16[256,1536]{1,0:T(8,128)(2,1)S(1)}, u32[]{:S(2)}, u32[]{:S(2)}) collective-permute-start(bf16[256,1536]{1,0:T(8,128)(2,1)S(1)} %add_convert_fusion.1), channel_id=1, source_target_pairs={{0,2},{2,0},{1,3},{3,1},{4,6},{6,4},{5,7},{7,5},{8,10},{10,8},{9,1... | collective-permute-start | bytes 2359304 | tf_op jit(solution)/shard_map/ppermute | solution.py:730
  202.7 13.9 %collective-permute-start.22 = (bf16[4,96,512]{2,1,0:T(8,128)(2,1)}, bf16[4,96,512]{2,1,0:T(8,128)(2,1)S(1)}, u32[]{:S(2)}, u32[]{:S(2)}) collective-permute-start(bf16[4,96,512]{2,1,0:T(8,128)(2,1)} %get-tuple-element.112), channel_id=1, source_target_pairs={{0,24},{8,0},{16,8},{24,16},{1,25},{9,1},{17,9},{25,17},{2,26},{10... | collective-permute-start | bytes 1179656 | tf_op jit(solution)/shard_map/ppermute | solution.py:730
  203.5 27.4 %collective-permute-start.19 = (bf16[4,96,640]{2,1,0:T(8,128)(2,1)}, bf16[4,96,640]{2,1,0:T(8,128)(2,1)S(1)}, u32[]{:S(2)}, u32[]{:S(2)}) collective-permute-start(bf16[4,96,640]{2,1,0:T(8,128)(2,1)} %get-tuple-element.108), channel_id=1, source_target_pairs={{0,96},{32,0},{64,32},{96,64},{1,97},{33,1},{65,33},{97,65},{2,98}... | collective-permute-start | bytes 1474568 | tf_op jit(solution)/shard_map/ppermute | solution.py:730
  204.6 26.3 %collective-permute-start.18 = (bf16[4,96,640]{2,1,0:T(8,128)(2,1)}, bf16[4,96,640]{2,1,0:T(8,128)(2,1)S(1)}, u32[]{:S(2)}, u32[]{:S(2)}) collective-permute-start(bf16[4,96,640]{2,1,0:T(8,128)(2,1)} %get-tuple-element.107), channel_id=1, source_target_pairs={{0,64},{32,96},{64,0},{96,32},{1,65},{33,97},{65,1},{97,33},{2,66}... | collective-permute-start | bytes 1474568 | tf_op jit(solution)/shard_map/ppermute | solution.py:730
  207.4 23.5 %collective-permute-start.17 = (bf16[4,96,640]{2,1,0:T(8,128)(2,1)}, bf16[4,96,640]{2,1,0:T(8,128)(2,1)S(1)}, u32[]{:S(2)}, u32[]{:S(2)}) collective-permute-start(bf16[4,96,640]{2,1,0:T(8,128)(2,1)} %get-tuple-element.106), channel_id=1, source_target_pairs={{0,32},{32,64},{64,96},{96,0},{1,33},{33,65},{65,97},{97,1},{2,34}... | collective-permute-start | bytes 1474568 | tf_op jit(solution)/shard_map/ppermute | solution.py:730
  208.1 22.7 %collective-permute-start.21 = (bf16[4,96,512]{2,1,0:T(8,128)(2,1)}, bf16[4,96,512]{2,1,0:T(8,128)(2,1)S(1)}, u32[]{:S(2)}, u32[]{:S(2)}) collective-permute-start(bf16[4,96,512]{2,1,0:T(8,128)(2,1)} %get-tuple-element.111), channel_id=1, source_target_pairs={{0,16},{8,24},{16,0},{24,8},{1,17},{9,25},{17,1},{25,9},{2,18},{10... | collective-permute-start | bytes 1179656 | tf_op jit(solution)/shard_map/ppermute | solution.py:730
  216.5 14.3 %collective-permute-start.20 = (bf16[4,96,512]{2,1,0:T(8,128)(2,1)}, bf16[4,96,512]{2,1,0:T(8,128)(2,1)S(1)}, u32[]{:S(2)}, u32[]{:S(2)}) collective-permute-start(bf16[4,96,512]{2,1,0:T(8,128)(2,1)} %get-tuple-element.110), channel_id=1, source_target_pairs={{0,8},{8,16},{16,24},{24,0},{1,9},{9,17},{17,25},{25,1},{2,10},{10... | collective-permute-start | bytes 1179656 | tf_op jit(solution)/shard_map/ppermute | solution.py:730
  236.0 22.6 %collective-permute-start.23 = (bf16[256,1536]{1,0:T(8,128)(2,1)S(1)}, bf16[256,1536]{1,0:T(8,128)(2,1)S(1)}, u32[]{:S(2)}, u32[]{:S(2)}) collective-permute-start(bf16[256,1536]{1,0:T(8,128)(2,1)S(1)} %copy-done.38), channel_id=1, source_target_pairs={{0,1},{1,0},{2,3},{3,2},{4,5},{5,4},{6,7},{7,6},{8,9},{9,8},{10,11... | collective-permute-start | bytes 2359304 | tf_op jit(solution)/shard_map/ppermute | solution.py:730
  236.1 12.3 %collective-permute-start.25 = (f32[8,1024]{1,0:T(8,128)S(1)}, f32[8,1024]{1,0:T(8,128)S(1)}, u32[]{:S(2)}, u32[]{:S(2)}) collective-permute-start(f32[8,1024]{1,0:T(8,128)S(1)} %copy-done.29), channel_id=1, source_target_pairs={{0,64},{32,96},{64,0},{96,32},{1,65},{33,97},{65,1},{97,33},{2,66}... | collective-permute-start | bytes 98312 | tf_op jit(solution)/shard_map/ppermute | solution.py:730
  237.2 12.7 %collective-permute-start.26 = (f32[8,1024]{1,0:T(8,128)S(1)}, f32[8,1024]{1,0:T(8,128)S(1)}, u32[]{:S(2)}, u32[]{:S(2)}) collective-permute-start(f32[8,1024]{1,0:T(8,128)S(1)} %copy-done.29), channel_id=1, source_target_pairs={{0,96},{32,0},{64,32},{96,64},{1,97},{33,1},{65,33},{97,65},{2,98}... | collective-permute-start | bytes 98312 | tf_op jit(solution)/shard_map/ppermute | solution.py:730
  244.8 19.3 %collective-permute-start.30 = (bf16[96,640]{1,0:T(8,128)(2,1)}, bf16[96,640]{1,0:T(8,128)(2,1)S(1)}, u32[]{:S(2)}, u32[]{:S(2)}) collective-permute-start(bf16[96,640]{1,0:T(8,128)(2,1)} %get-tuple-element.129), channel_id=1, source_target_pairs={{0,24},{8,0},{16,8},{24,16},{1,25},{9,1},{17,9},{25,17},{2,26},{10... | collective-permute-start | bytes 368648 | tf_op jit(solution)/shard_map/ppermute | solution.py:730
  248.4 15.8 %collective-permute-start.29 = (bf16[96,640]{1,0:T(8,128)(2,1)}, bf16[96,640]{1,0:T(8,128)(2,1)S(1)}, u32[]{:S(2)}, u32[]{:S(2)}) collective-permute-start(bf16[96,640]{1,0:T(8,128)(2,1)} %get-tuple-element.128), channel_id=1, source_target_pairs={{0,16},{8,24},{16,0},{24,8},{1,17},{9,25},{17,1},{25,9},{2,18},{10... | collective-permute-start | bytes 368648 | tf_op jit(solution)/shard_map/ppermute | solution.py:730
  249.9 14.3 %collective-permute-start.28 = (bf16[96,640]{1,0:T(8,128)(2,1)}, bf16[96,640]{1,0:T(8,128)(2,1)S(1)}, u32[]{:S(2)}, u32[]{:S(2)}) collective-permute-start(bf16[96,640]{1,0:T(8,128)(2,1)} %get-tuple-element.127), channel_id=1, source_target_pairs={{0,8},{8,16},{16,24},{24,0},{1,9},{9,17},{17,25},{25,1},{2,10},{10... | collective-permute-start | bytes 368648 | tf_op jit(solution)/shard_map/ppermute | solution.py:730
  269.6 8.0 %collective-permute-start.35 = (f32[8,1024]{1,0:T(8,128)S(1)}, f32[8,1024]{1,0:T(8,128)S(1)}, u32[]{:S(2)}, u32[]{:S(2)}) collective-permute-start(f32[8,1024]{1,0:T(8,128)S(1)} %add_add_fusion.2), channel_id=1, source_target_pairs={{0,24},{8,0},{16,8},{24,16},{1,25},{9,1},{17,9},{25,17},{2,26},{10... | collective-permute-start | bytes 98312 | tf_op jit(solution)/shard_map/ppermute | solution.py:730
  270.8 6.8 %collective-permute-start.36 = (f32[8,1024]{1,0:T(8,128)S(1)}, f32[8,1024]{1,0:T(8,128)S(1)}, u32[]{:S(2)}, u32[]{:S(2)}) collective-permute-start(f32[8,1024]{1,0:T(8,128)S(1)} %add_add_fusion.2), channel_id=1, source_target_pairs={{0,8},{8,16},{16,24},{24,0},{1,9},{9,17},{17,25},{25,1},{2,10},{10... | collective-permute-start | bytes 98312 | tf_op jit(solution)/shard_map/ppermute | solution.py:730
  271.7 32.4 %collective-permute-start.16 = (bf16[256,1536]{1,0:T(8,128)(2,1)}, bf16[256,1536]{1,0:T(8,128)(2,1)S(1)}, u32[]{:S(2)}, u32[]{:S(2)}) collective-permute-start(bf16[256,1536]{1,0:T(8,128)(2,1)} %get-tuple-element.115), channel_id=1, source_target_pairs={{0,1},{1,0},{2,3},{3,2},{4,5},{5,4},{6,7},{7,6},{8,9},{9,8},{10,11... | collective-permute-start | bytes 2359304 | tf_op jit(solution)/shard_map/ppermute | solution.py:730
  271.7 7.5 %collective-permute-start.42 = (bf16[48,1152]{1,0:T(8,128)(2,1)}, bf16[48,1152]{1,0:T(8,128)(2,1)S(1)}, u32[]{:S(2)}, u32[]{:S(2)}) collective-permute-start(bf16[48,1152]{1,0:T(8,128)(2,1)} %get-tuple-element.145), channel_id=1, source_target_pairs={{0,4},{4,0},{1,5},{5,1},{2,6},{6,2},{3,7},{7,3},{8,12},{12,8},{9,1... | collective-permute-start | bytes 331784 | tf_op jit(solution)/shard_map/ppermute | solution.py:730
  274.0 30.1 %collective-permute-start.24 = (bf16[256,1536]{1,0:T(8,128)(2,1)}, bf16[256,1536]{1,0:T(8,128)(2,1)}, u32[]{:S(2)}, u32[]{:S(2)}) collective-permute-start(bf16[256,1536]{1,0:T(8,128)(2,1)} %add_convert_fusion), channel_id=1, source_target_pairs={{0,2},{2,0},{1,3},{3,1},{4,6},{6,4},{5,7},{7,5},{8,10},{10,8},{9,1... | collective-permute-start | bytes 2359304 | tf_op jit(solution)/shard_map/ppermute | solution.py:730
  277.6 17.9 %collective-permute-start.37 = (f32[8,1024]{1,0:T(8,128)S(1)}, f32[8,1024]{1,0:T(8,128)S(1)}, u32[]{:S(2)}, u32[]{:S(2)}) collective-permute-start(f32[8,1024]{1,0:T(8,128)S(1)} %add_add_fusion.1), channel_id=1, source_target_pairs={{0,4},{4,0},{1,5},{5,1},{2,6},{6,2},{3,7},{7,3},{8,12},{12,8},{9,1... | collective-permute-start | bytes 98312 | tf_op jit(solution)/shard_map/ppermute | solution.py:730
  280.2 18.6 %collective-permute-start.43 = (f32[12,256]{1,0:T(8,128)S(1)}, f32[12,256]{1,0:T(8,128)S(1)}, u32[]{:S(2)}, u32[]{:S(2)}) collective-permute-start(f32[12,256]{1,0:T(8,128)S(1)} %get-tuple-element.205), channel_id=1, source_target_pairs={{0,1},{1,0},{2,3},{3,2},{4,5},{5,4},{6,7},{7,6},{8,9},{9,8},{10,11... | collective-permute-start | bytes 36872 | tf_op jit(solution)/shard_map/ppermute | solution.py:746
  280.3 27.2 %collective-permute-start.13 = (bf16[256,1536]{1,0:T(8,128)(2,1)}, bf16[256,1536]{1,0:T(8,128)(2,1)}, u32[]{:S(2)}, u32[]{:S(2)}) collective-permute-start(bf16[256,1536]{1,0:T(8,128)(2,1)} %get-tuple-element.89), channel_id=1, source_target_pairs={{0,1},{1,0},{2,3},{3,2},{4,5},{5,4},{6,7},{7,6},{8,9},{9,8},{10,11... | collective-permute-start | bytes 2359304 | tf_op jit(solution)/shard_map/ppermute | solution.py:730
  (57 other events, 567.0 us)
Sparse Core Ops, SparseCore 0:
  27.3 71.2 all-gather.1
  160.3 92.3 reduce-scatter.1
